TPU v7x, 256 devices: a whole 4x4x8 slice. The times are simulated.
256 devices in a mesh: user: 4 (over x), seq: 64 (over z, y, core).
Axes of the slice: x: 4, y: 4, z: 8, core: 2. Of those that a mesh axis runs over, the one named last changes fastest.
Arguments:
- interaction_memory: bfloat16 [8, 32768, 1024], P('user', 'seq'), may hold values from -6 to 6
- contender_embeddings: bfloat16 [8, 8192, 1024], P('user', 'seq'), may hold values from -6 to 6
- contender_projection_matrix: bfloat16 [1024, 2048], replicated, may hold values from -0.1875 to 0.1875
- memory_projection_matrix: bfloat16 [1024, 2048], P(None, 'user'), may hold values from -0.1875 to 0.1875
- coarse_projection_matrix: bfloat16 [1024, 1024], replicated, may hold values from -0.1875 to 0.1875
- averaged_memory_matrix: bfloat16 [1024, 512], replicated, may hold values from -0.1875 to 0.1875
- finalist_indices: int32 [8, 256], P('user'), may hold values from -1 to 8191, as said below
- memory_extents: int32 [8], P('user'), may hold values from 2048 to 32768
Outputs:
- coarse_ratings: float32 [8, 8192], P('user', 'seq')
- fine_layer_result: bfloat16 [8, 8192, 1024], P('user', 'seq')
Inputs may be any that keep to these rules, and one draw needn't show every extreme that they name: `finalist_indices`: within a user the indices are distinct. At most 8 of one user's survivors lie among the 128 candidates of one index of seq, and exactly 8 do for some index, for every user. For every even index i of seq, at most 8 of one user's survivors lie among the candidates of indices i and i + 1 together.
All inputs are finite; a program needn't handle non-finite values.
Results may differ from a plain program's by a relative error of at most 0.0036.
Values may be sent and summed in bfloat16 or wider, within the bound.
A program may use at most 64 MiB of HBM per device.

v0:
```python
import math

import jax
import jax.numpy as jnp
from jax import lax
from jax.sharding import PartitionSpec as P

HEADS = 16


epsilon = 1e-05


def local(
    interaction_memory,
    contender_embeddings,
    contender_projection_matrix,
    memory_projection_matrix,
    coarse_projection_matrix,
    averaged_memory_matrix,
    finalist_indices,
    memory_extents,
):
    members, hist_rows, width = interaction_memory.shape
    contender_entries = contender_embeddings.shape[1]
    hidden_width = averaged_memory_matrix.shape[1]
    holding_participants = lax.axis_size("seq")
    capacity_ceiling = 2 * finalist_indices.shape[1] // holding_participants
    head_dim = width // HEADS
    entry_offset = lax.axis_index("seq")
    places = entry_offset * hist_rows + jnp.arange(hist_rows, dtype=jnp.int32)
    live = (places[None, :] < memory_extents[:, None]).astype(jnp.float32)
    column_sum = jnp.einsum(
        "bj,bjd->bd",
        live.astype(jnp.bfloat16),
        interaction_memory,
        preferred_element_type=jnp.float32,
    )
    partial_pool = jnp.dot(
        column_sum, averaged_memory_matrix.astype(jnp.float32), precision=lax.Precision.HIGHEST
    )
    pooled = lax.psum(partial_pool, "seq") / jnp.sqrt(memory_extents.astype(jnp.float32))[:, None]
    gate_up = jnp.einsum(
        "bcd,de->bce",
        contender_embeddings,
        coarse_projection_matrix,
        preferred_element_type=jnp.float32,
    )
    pre_hidden = jax.nn.silu(gate_up[..., :hidden_width]) * gate_up[..., hidden_width:]
    coarse_ratings = jnp.einsum(
        "bce,be->bc", pre_hidden, pooled, precision=lax.Precision.HIGHEST
    ) / math.sqrt(hidden_width)
    piece = lax.all_gather(memory_projection_matrix, "user", axis=1, tiled=True)
    raw = jnp.einsum("bjd,de->bje", interaction_memory, piece, preferred_element_type=jnp.float32)
    columns = jnp.arange(piece.shape[1])
    projected = jnp.where(columns < width, jax.nn.silu(raw), raw).astype(jnp.bfloat16)
    keys = projected[..., :width].reshape(members, hist_rows, HEADS, head_dim)
    values = projected[..., width:].reshape(members, hist_rows, HEADS, head_dim)
    participant_private = finalist_indices - entry_offset * contender_entries
    belonging_to_participant = (
        (finalist_indices >= 0)
        & (participant_private >= 0)
        & (participant_private < contender_entries)
    )
    matches = belonging_to_participant[:, :, None] & (
        participant_private[:, :, None] == jnp.arange(contender_entries)[None, None, :]
    )
    flagged = jnp.any(matches, axis=1).astype(jnp.int32)
    placing = jnp.cumsum(flagged, axis=1) - flagged
    select = (
        (flagged[:, None, :] == 1)
        & (placing[:, None, :] == jnp.arange(capacity_ceiling)[None, :, None])
    ).astype(jnp.bfloat16)
    chosen_rows = jnp.einsum(
        "brc,bcd->rbd", select, contender_embeddings, preferred_element_type=jnp.float32
    ).astype(jnp.bfloat16)
    lifted = jax.nn.silu(
        jnp.einsum(
            "rbd,de->rbe",
            chosen_rows,
            contender_projection_matrix,
            preferred_element_type=jnp.float32,
        )
    )
    gates = lifted[..., :width]
    queries = lifted[..., width:].astype(jnp.bfloat16)
    block = lax.all_gather(queries, "seq", axis=0, tiled=True)
    count = block.shape[0]
    results = []
    for member in range(members):
        query_heads = block[:, member].reshape(count, HEADS, head_dim)
        logits = jnp.einsum(
            "rhd,jhd->hrj", query_heads, keys[member], preferred_element_type=jnp.float32
        ) / math.sqrt(head_dim)
        weights = (jax.nn.silu(logits) * live[member][None, None, :]).astype(jnp.bfloat16)
        summed = jnp.einsum(
            "hrj,jhd->rhd", weights, values[member], preferred_element_type=jnp.float32
        )
        results.append(summed.reshape(count, width))
    terms = jnp.stack(results, axis=1)
    totals = lax.psum(terms, "seq")
    attention = lax.dynamic_slice_in_dim(
        totals, entry_offset * capacity_ceiling, capacity_ceiling, 0
    )
    mean = jnp.mean(attention, axis=-1, keepdims=True)
    centred = attention - mean
    variance = jnp.mean(centred * centred, axis=-1, keepdims=True)
    normed = centred / jnp.sqrt(variance + epsilon)
    mixed_rows = (normed * gates + chosen_rows.astype(jnp.float32)).astype(jnp.bfloat16)
    fine_layer_result = jnp.einsum(
        "brc,rbd->bcd", select, mixed_rows, preferred_element_type=jnp.float32
    ).astype(jnp.bfloat16)
    return (coarse_ratings, fine_layer_result)


def solution(mesh):
    placed = (
        P("user", "seq", None),
        P("user", "seq", None),
        P(),
        P(None, "user"),
        P(),
        P(),
        P("user", None),
        P("user"),
    )
    return jax.shard_map(
        local,
        mesh=mesh,
        in_specs=placed,
        out_specs=(P("user", "seq"), P("user", "seq", None)),
        check_vma=False,
    )
```

profile of v0, /device:TPU:1, one launch (start us, length us, event | category | flops | bytes accessed | tf_op | source)
XLA Modules:
  0.0 400.7 jit_solution(11846647728723384411)
XLA Ops:
  7.2 0.0 copy-start
  7.2 0.0 copy-start.2
  7.2 0.0 all-gather.5.cloned.1.call-start
  7.2 0.8 broadcast_subtract_fusion
  8.1 0.7 compare_and_fusion
  8.8 0.2 fusion.21
  9.0 0.3 reduce_window_sum.11
  9.3 1.2 fusion.11
  10.5 2.9 divide_multiply_fusion
  13.4 0.6 slice.84
  14.0 0.0 all-gather.5.cloned.1.call-update
  14.0 0.0 all-gather.3.cloned.1.call-start
  14.1 0.7 all-gather.3.cloned.1.call-update
  14.8 0.0 all-reduce.2.cloned.1.call-start
  14.9 0.0 copy-done.2
  14.9 0.1 compare_convert_fusion
  14.9 80.7 %all-gather.5.cloned.1.call-done = bf16[512,2,1024]{2,0,1:T(8,128)(2,1)} async-done(((bf16[8,2,1024]{2,0,1:T(8,128)(2,1)}), bf16[512,2,1024]{2,0,1:T(8,128)(2,1)}) %all-gather.5.cloned.1.call-update) | async-done | bytes 2097168 | tf_op jit(solution)/shard_map/all_gather | solution.py:87
  95.7 2.7 fusion.49
  98.4 2.3 copy.30
  100.7 1.3 copy.27
  102.0 43.5 %all-gather.3.cloned.1.call-done = bf16[1024,2048]{1,0:T(8,128)(2,1)} async-done(((bf16[1024,512]{1,0:T(8,128)(2,1)}), bf16[1024,2048]{1,0:T(8,128)(2,1)}) %all-gather.3.cloned.1.call-update) | async-done | bytes 4194320 | tf_op jit(solution)/shard_map/all_gather | solution.py:53
  145.5 0.0 copy-done
  145.5 7.8 %fusion = bf16[2,512,2048]{2,1,0:T(8,128)(2,1)S(1)} fusion(pred[2048]{0:T(1024)(128)(4,1)S(1)} %iota_compare_fusion.1, bf16[2,512,1024]{2,1,0:T(8,128)(2,1)S(1)} %copy-done, bf16[1024,2048]{1,0:T(8,128)(2,1)} %all-gather.3.cloned.1.call-done), kind=kOutput, calls=%fused_computation.3 | convolution fusion | flops 4307550208 | bytes 10487808 | tf_op jit(solution)/shard_map/bjd,de->bje/dot_general | solution.py:54
  153.3 1.8 fusion.48
  155.2 2.3 copy.29
  157.4 2.3 copy.31
  159.7 10.8 %fusion.6 = f32[16,64,512]{2,1,0:T(8,128)} fusion(bf16[512,16,64]{0,2,1:T(8,128)(2,1)} %bitcast.55, bf16[512,16,64]{0,2,1:T(8,128)(2,1)} %bitcast.53, bf16[512,16,64]{0,2,1:T(8,128)(2,1)} %bitcast.57, f32[512]{0:T(512)S(1)} %bitcast.59), kind=kOutput, calls=%fused_computation.10 | convolution fusion | flops 1103101952 | bytes 5244928 | tf_op jit(solution)/shard_map/hrj,jhd->rhd/dot_general | solution.py:96
  170.6 2.9 copy.33
  173.5 2.3 copy.26
  175.8 1.3 copy.28
  177.1 10.8 %fusion.5 = f32[16,64,512]{2,1,0:T(8,128)} fusion(bf16[512,16,64]{0,2,1:T(8,128)(2,1)} %bitcast.54, bf16[512,16,64]{0,2,1:T(8,128)(2,1)} %bitcast.52, bf16[512,16,64]{0,2,1:T(8,128)(2,1)} %bitcast.56, f32[512]{0:T(512)S(1)} %bitcast.58), kind=kOutput, calls=%fused_computation.9 | convolution fusion | flops 1103101952 | bytes 5244928 | tf_op jit(solution)/shard_map/hrj,jhd->rhd/dot_general | solution.py:96
  187.9 2.9 copy.32
  190.8 4.7 %pad_maximum_fusion = f32[512,2,1024]{2,0,1:T(8,128)} fusion(f32[512,1,1024]{2,0,1:T(8,128)} %copy.33, f32[512,1,1024]{2,0,1:T(8,128)} %copy.32), kind=kLoop, calls=%fused_computation.4 | loop fusion | flops 1048576 | bytes 8388608 | tf_op jit(solution)/shard_map/stack | solution.py:100
  195.5 0.0 copy-start.1
  195.5 0.0 all-reduce.2.cloned.1.call-update
  195.6 0.4 fusion.36
  195.9 1.7 fusion.29
  197.7 124.8 %psum.14 = f32[2,512]{1,0:T(2,128)S(1)} all-reduce(f32[2,512]{1,0:T(2,128)S(1)} %fusion.29), channel_id=1, replica_groups=mesh['user'=4,'seq'=64] {'seq'}, use_global_device_ids=true, to_apply=%region_0.0 | all-reduce | flops 1024 | bytes 8192 | tf_op jit(solution)/shard_map/psum | solution.py:42
  322.5 0.1 divide_bitcast_fusion
  322.6 0.0 copy-done.1
  322.6 2.3 fusion.7
  324.9 0.7 fusion.12
  325.5 0.6 broadcast_multiply_fusion.1
  326.1 64.1 %all-reduce.2.cloned.1.call-done = f32[512,2,1024]{2,0,1:T(8,128)} async-done(((f32[512,2,1024]{2,0,1:T(8,128)}), f32[512,2,1024]{2,0,1:T(8,128)}) %all-reduce.2.cloned.1.call-update) | async-done | bytes 4194320 | tf_op jit(solution)/shard_map/psum | solution.py:101
  390.2 0.9 dynamic-slice_reduce_fusion
  391.2 1.0 multiply_reduce_fusion
  392.2 2.0 convolution_convert_fusion
  (8 shorter events, 0.1 us)
Async XLA Ops:
  7.2 138.4 %copy-start = (bf16[2,512,1024]{2,1,0:T(8,128)(2,1)S(1)}, bf16[2,512,1024]{2,1,0:T(8,128)(2,1)}, u32[]{:S(2)}) copy-start(bf16[2,512,1024]{2,1,0:T(8,128)(2,1)} %param.8) | copy-start | bytes 6291460
  7.2 7.7 %copy-start.2 = (s32[2]{0:T(128)S(1)}, s32[2]{0:T(128)}, u32[]{:S(2)}) copy-start(s32[2]{0:T(128)} %param.15) | copy-start | bytes 28
  7.2 88.5 %all-gather.5.cloned.1.call-start = ((), (), s32[]{:S(2)}) async-start(), calls=%async_computation.1 | async-start | bytes 2129920 | tf_op jit(solution)/shard_map/all_gather | solution.py:87
  14.0 131.5 %all-gather.3.cloned.1.call-start = ((), (), s32[]{:S(2)}) async-start(), calls=%async_computation | async-start | bytes 5242880 | tf_op jit(solution)/shard_map/all_gather | solution.py:53
  14.8 375.4 %all-reduce.2.cloned.1.call-start = ((), (), s32[]{:S(2)}) async-start(), calls=%async_computation.2 | async-start | bytes 8388608 | tf_op jit(solution)/shard_map/psum | solution.py:101
  195.5 127.0 %copy-start.1 = (bf16[2,128,1024]{2,1,0:T(8,128)(2,1)S(1)}, bf16[2,128,1024]{2,1,0:T(8,128)(2,1)}, u32[]{:S(2)}) copy-start(bf16[2,128,1024]{2,1,0:T(8,128)(2,1)} %param.9) | copy-start | bytes 1572868
Sparse Core Ops, SparseCore 0:
  14.2 81.4 all-gather.4
  97.5 48.0 all-gather.2
  195.7 194.5 all-reduce.1
where the time goes:
time: 402 us; the launch traced here: 401 us
  waiting for transfers between devices  189 us (47%)
  blocking collectives  125 us (31%)
  matrix products  40.6 us (10%)
  local copies, waits for them, and re-layouts  22.9 us (6%)
  between operations  13.8 us (3%)
  other arithmetic  9.48 us (2%)
    psum x1, blocking collectives, local(): lax.psum(partial_pool, 'seq')  125 us
    all_gather x1, waiting for transfers between devices, local(): block = lax.all_gather(queries, 'seq', axis=0, tiled=True)  80.7 us
    psum x1, waiting for transfers between devices, local(): totals = lax.psum(terms, 'seq')  64.1 us
    all_gather x1, waiting for transfers between devices, local(): piece = lax.all_gather(memory_projection_matrix, 'user', axis=1, tiled=True)  43.5 us
    dot_general x2, matrix products, local(): jnp.einsum('hrj,jhd->rhd', weights, values[member], preferred_element_typ...  21.6 us
  transfers between devices with their start and end apart: 3, of which 3 were waited for; matrix products, arithmetic and copies ran while one was open for 3% of the time, Pallas kernels for 0%

commit v1 on v0

v1 whole, which is shorter than its diff:
```python
import functools
import math

import jax
import jax.numpy as jnp
from jax import lax
from jax.experimental import pallas as pl
from jax.experimental.pallas import tpu as pltpu
from jax.sharding import PartitionSpec as P

HEADS = 16
CORES = 2
YS = 4
XS = 4
CHUNKS = 4
LANES = 128
SLOTS = 8
epsilon = 1e-05

F32 = jnp.float32
BF16 = jnp.bfloat16
MESH = pl.DeviceIdType.MESH


def dot(a, b):
    return jnp.dot(a, b, preferred_element_type=F32)


def dot_nt(a, b):
    return lax.dot_general(a, b, (((1,), (1,)), ((), ())), preferred_element_type=F32)


def silu(x):
    h = x * 0.5
    return h + h * jnp.tanh(h)


def kernel(
    zs,
    m_hbm, cand_hbm, wc_hbm, wm_hbm, wco_hbm, avg_hbm, idx_ref, ext_ref,
    coarse_ref, fine_ref,
    cand, wq, wg, wco, avg, mall, wbuf,
    xbuf, xrow, gates, sel, selt,
    qbuf, q2, kbuf, vbuf, pf, psend, pown, yrecv, zown, zsend, zrecv, afull,
    pre, cs, csy, csz, pool,
    local_sem, wl_sem, m_sem, x_sem, wx_send, wx_recv, wf_send, wf_recv,
    qz_send, qz_recv, qy_send, qy_recv,
    cy_send, cy_recv, cz_send, cz_recv, cp_sem,
    py_send, py_recv, pz_send, pz_recv, a_sem,
):
    u = lax.axis_index("user")
    s = lax.axis_index("seq")
    c = s % CORES
    y = (s // CORES) % YS
    z = s // (CORES * YS)
    chip = s // CORES
    hist = m_hbm.shape[1]
    half = wq.shape[1]
    colour = (y + 2 * z) % CHUNKS

    def at(x_, z_, y_, c_):
        return (x_, (z_ * YS + y_) * CORES + c_)

    sibling = at(u, z, y, 1 - c)

    def xpeer(d):
        return at((u + d) % XS, z, y, c)

    def ypeer(d):
        return at(u, z, (y + d) % YS, c)

    def zpeer(d):
        return at(u, (z + d) % zs, y, c)

    def lanes(start, size):
        return pl.ds(pl.multiple_of(start, LANES), size)

    def remote(src, dst, send, recv, device):
        return pltpu.make_async_remote_copy(
            src_ref=src, dst_ref=dst, send_sem=send, recv_sem=recv,
            device_id=device, device_id_type=MESH,
        )

    l_cand = pltpu.make_async_copy(cand_hbm, cand, local_sem.at[0])
    l_wq = pltpu.make_async_copy(
        wc_hbm.at[:, lanes(2 * half + c * half, half)], wq, local_sem.at[1]
    )
    l_m = pltpu.make_async_copy(m_hbm, mall.at[c], local_sem.at[2])
    l_wg = pltpu.make_async_copy(wc_hbm.at[:, pl.ds(0, 2 * half)], wg, local_sem.at[3])
    l_wco = pltpu.make_async_copy(wco_hbm, wco, local_sem.at[4])
    l_avg = pltpu.make_async_copy(
        avg_hbm.at[pl.ds(pl.multiple_of(c * half, half), half), :], avg, local_sem.at[5]
    )
    l_cand.start()
    l_wq.start()

    barrier = pltpu.get_barrier_semaphore()

    def greet(device):
        pl.semaphore_signal(barrier, inc=1, device_id=device, device_id_type=MESH)

    greet(sibling)
    for d in range(1, XS):
        greet(xpeer(d))
    for d in range(1, YS):
        greet(ypeer(d))
    for d in range(1, zs):
        greet(zpeer(d))

    l_m.start()
    l_wg.start()
    l_wco.start()
    l_avg.start()

    own_kv = u // 2
    holds = (u % 2) == c

    def wl_copy(q):
        return pltpu.make_async_copy(
            wm_hbm.at[:, lanes(q * LANES, LANES)], wbuf.at[q, own_kv], wl_sem.at[q]
        )

    @pl.when(holds)
    def _():
        for q in range(CHUNKS):
            wl_copy(q).start()

    rows16 = 2 * SLOTS
    ones = jnp.ones((rows16, idx_ref.shape[1]), BF16)
    pair = 2 * cand_hbm.shape[1]
    mine = cand_hbm.shape[1]
    upper = jnp.where(
        lax.broadcasted_iota(jnp.int32, (pair, pair), 0)
        < lax.broadcasted_iota(jnp.int32, (pair, pair), 1),
        1.0, 0.0,
    ).astype(BF16)
    eye = jnp.where(
        lax.broadcasted_iota(jnp.int32, (mine, mine), 0)
        == lax.broadcasted_iota(jnp.int32, (mine, mine), 1),
        1.0, 0.0,
    ).astype(BF16)
    row = lax.broadcasted_iota(jnp.int32, (rows16, pair), 0)
    for b in range(2):
        near = idx_ref[b:b + 1, :] - chip * pair
        matches = jnp.where(
            lax.broadcasted_iota(jnp.int32, (pair, idx_ref.shape[1]), 0) == near, 1.0, 0.0
        ).astype(BF16)
        flagged = dot_nt(ones, matches)
        placing = dot(flagged.astype(BF16), upper)
        target = (row - b * SLOTS).astype(F32)
        chosen = jnp.where((flagged > 0.5) & (jnp.abs(placing - target) < 0.5), 1.0, 0.0)
        chosen = jnp.where((row // SLOTS) == b, chosen, 0.0)
        own = jnp.where(c == 0, chosen[:, :mine], chosen[:, mine:]).astype(BF16)
        sel[b] = own
        selt[b] = dot_nt(eye, own).astype(BF16)

    l_cand.wait()
    found = dot(sel[0], cand[0]) + dot(sel[1], cand[1])
    xrow[...] = found.astype(BF16)

    pl.semaphore_wait(barrier, 1 + (XS - 1) + (YS - 1) + (zs - 1))

    x_copy = remote(xrow, xbuf, x_sem.at[0], x_sem.at[1], sibling)
    x_copy.start()

    def wx_copy(d):
        return remote(
            wm_hbm.at[:, lanes(colour * LANES, LANES)], wbuf.at[colour, own_kv],
            wx_send.at[d - 1], wx_recv.at[own_kv], xpeer(d),
        )

    @pl.when(holds)
    def _():
        for d in (1, 3, 2):
            wx_copy(d).start()

    x_copy.wait_recv()
    rows = xrow[...].astype(F32) + xbuf[...].astype(F32)
    xrow2 = rows.astype(BF16)
    l_wq.wait()
    queries = silu(dot(xrow2, wq[...])).astype(BF16)
    qbuf[y, z] = (queries.astype(F32) * (0.5 / math.sqrt(2 * half // HEADS))).astype(BF16)

    def qz_copy(d):
        return remote(qbuf.at[y, z], qbuf.at[y, z], qz_send.at[d - 1], qz_recv.at[d - 1], zpeer(d))

    for d in range(1, zs):
        qz_copy(d).start()
    m_copy = remote(m_hbm, mall.at[c], m_sem.at[0], m_sem.at[1], sibling)
    m_copy.start()

    l_wg.wait()
    gates[...] = silu(dot(xrow2, wg[...]))

    depth = wbuf.shape[2] // 2

    def wf_copies(kv):
        block = wbuf.at[colour, kv]
        low = wbuf.at[colour, kv, pl.ds(0, depth)]
        high = wbuf.at[colour, kv, pl.ds(depth, depth)]
        return (
            remote(block, block, wf_send.at[kv, 0], wf_recv.at[kv, 0], ypeer(1)),
            remote(block, block, wf_send.at[kv, 1], wf_recv.at[kv, 1], ypeer(YS - 1)),
            remote(low, low, wf_send.at[kv, 2], wf_recv.at[kv, 2], zpeer(1)),
            remote(high, high, wf_send.at[kv, 3], wf_recv.at[kv, 3], zpeer(zs - 1)),
        )

    def wx_wait(kv):
        block = wbuf.at[colour, kv]
        remote(block, block, wx_send.at[0], wx_recv.at[kv], xpeer(1)).wait_recv()

    def forward(kv):
        @pl.when(c + 2 * kv != u)
        def _():
            wx_wait(kv)
            for copy in wf_copies(kv):
                copy.start()

    forward(0)
    forward(1)

    for d in range(1, zs):
        qz_copy(d).wait_recv()

    def qy_copy(d):
        return remote(qbuf.at[y], qbuf.at[y], qy_send.at[d - 1], qy_recv.at[d - 1], ypeer(d))

    for d in range(1, YS):
        qy_copy(d).start()

    l_wco.wait()
    for b in range(2):
        hidden = dot(cand[b], wco[...])
        pre[b] = silu(hidden[:, :half]) * hidden[:, half:]

    l_m.wait()
    m_copy.wait_recv()
    live_row = lax.broadcasted_iota(jnp.int32, (rows16, hist), 0)
    live_col = lax.broadcasted_iota(jnp.int32, (rows16, hist), 1)
    total = jnp.zeros((rows16, half), F32)
    for b in range(2):
        for core in range(CORES):
            place = (chip * CORES + core) * hist + live_col
            mask = jnp.where((live_row == b) & (place < ext_ref[b]), 1.0, 0.0).astype(BF16)
            total = total + dot(mask, mall[core, b, :, lanes(c * half, half)])
    cs[0] = total[:8]

    def cy_copy(d):
        return remote(cs.at[0], csy.at[d - 1], cy_send.at[d - 1], cy_recv.at[d - 1], ypeer(d))

    def cz_copy(d):
        return remote(cs.at[1], csz.at[d - 1], cz_send.at[d - 1], cz_recv.at[d - 1], zpeer(d))

    for d in range(1, YS):
        cy_copy(d).start()

    for d in range(1, YS):
        qy_copy(d).wait_recv()
    for yy in range(YS):
        block = qbuf[yy].astype(F32)
        for b in range(2):
            part = block[:, b * SLOTS:(b + 1) * SLOTS, :].reshape(zs * SLOTS, half)
            q2[b, yy * zs * SLOTS:(yy + 1) * zs * SLOTS, :] = part.astype(BF16)

    for d in range(1, YS):
        cy_copy(d).wait_recv()
    cs[1] = cs[0] + (csy[0] + csy[1] + csy[2])
    for d in range(1, zs):
        cz_copy(d).start()

    def py_copy(q, d):
        return remote(
            psend.at[q, (y + d) % YS], yrecv.at[q, d - 1],
            py_send.at[q, d - 1], py_recv.at[q, d - 1], ypeer(d),
        )

    def pz_copy(q, d):
        return remote(
            zsend.at[q, (z + d) % zs], zrecv.at[q, d - 1],
            pz_send.at[q, d - 1], pz_recv.at[q, d - 1], zpeer(d),
        )

    lane = lax.broadcasted_iota(jnp.int32, (YS * zs * SLOTS, LANES), 1)
    first = lane < (LANES // 2)
    spot = lax.broadcasted_iota(jnp.int32, (hist, LANES), 0)

    def w_wait(q, kv):
        near = (q - colour + CHUNKS) % CHUNKS
        local_ = c + 2 * kv == u

        @pl.when(local_)
        def _():
            wl_copy(q).wait()

        @pl.when(jnp.logical_not(local_))
        def _():
            copies = wf_copies(kv)

            @pl.when(near == 1)
            def _():
                copies[1].wait_recv()

            @pl.when(near == 3)
            def _():
                copies[0].wait_recv()

            @pl.when(near == 2)
            def _():
                copies[2].wait_recv()
                copies[3].wait_recv()

    def compute(q):
        w_wait(q, 0)
        w_wait(q, 1)

        def project(i, carry):
            b, core = i // CORES, i % CORES
            weights = jnp.concatenate([wbuf[q, 0], wbuf[q, 1]], axis=1)
            raw = dot(mall[core, b], weights)
            at_rows = pl.ds(pl.multiple_of(core * hist, hist), hist)
            kbuf[b, at_rows, :] = silu(raw[:, :LANES]).astype(BF16)
            place = (chip * CORES + core) * hist + spot
            vbuf[b, at_rows, :] = jnp.where(place < ext_ref[b], raw[:, LANES:], 0.0).astype(BF16)
            return carry

        lax.fori_loop(0, 2 * CORES, project, 0)

        for b in range(2):
            queries_ = q2[b, :, lanes(q * LANES, LANES)]
            outs = []
            for h in range(2):
                keep = first if h == 0 else jnp.logical_not(first)
                masked = jnp.where(keep, queries_.astype(F32), 0.0).astype(BF16)
                logits = dot_nt(masked, kbuf[b])
                weights = (logits + logits * jnp.tanh(logits)).astype(BF16)
                outs.append(dot(weights, vbuf[b]))
            out = jnp.where(first, outs[0], outs[1])
            pf[:, :, b * SLOTS:(b + 1) * SLOTS, :] = out.reshape(YS, zs, SLOTS, LANES)
        psend[q] = pf[...].astype(BF16)
        pown[q] = pf[y]
        for d in range(1, YS):
            py_copy(q, d).start()

    def reduce_y(q):
        for d in range(1, YS):
            py_copy(q, d).wait_recv()
        total_ = pown[q]
        for d in range(1, YS):
            total_ = total_ + yrecv[q, d - 1].astype(F32)
        pown[q] = total_
        zsend[q] = total_.astype(BF16)
        zown[q] = pown[q, z]
        for d in range(1, zs):
            pz_copy(q, d).start()

    def step(q, carry):
        @pl.when(q < CHUNKS)
        def _():
            compute(q)

        @pl.when(q > 0)
        def _():
            reduce_y(q - 1)

        return carry

    lax.fori_loop(0, CHUNKS + 1, step, 0)

    for d in range(1, zs):
        cz_copy(d).wait_recv()
    summed = cs[1]
    for d in range(1, zs):
        summed = summed + csz[d - 1]
    l_avg.wait()
    part1 = summed.astype(BF16)
    rest = summed - part1.astype(F32)
    part2 = rest.astype(BF16)
    part3 = (rest - part2.astype(F32)).astype(BF16)
    pool[0] = dot(part1, avg[...]) + dot(part2, avg[...]) + dot(part3, avg[...])
    cp_copy = remote(pool.at[0], pool.at[1], cp_sem.at[0], cp_sem.at[1], sibling)
    cp_copy.start()

    def reduce_z(q, carry):
        total_ = zown[q]
        for d in range(1, zs):
            pz_copy(q, d).wait_recv()
            total_ = total_ + zrecv[q, d - 1].astype(F32)
        afull[c, q] = total_
        return carry

    lax.fori_loop(0, CHUNKS, reduce_z, 0)
    a_copy = remote(afull.at[c], afull.at[c], a_sem.at[0], a_sem.at[1], sibling)
    a_copy.start()

    cp_copy.wait_recv()
    pooled = pool[0] + pool[1]
    for b in range(2):
        scale = 1.0 / (
            jnp.sqrt(jnp.full((8, LANES), ext_ref[b], jnp.int32).astype(F32)) * math.sqrt(half)
        )
        scores = lax.dot_general(
            pooled, pre[b], (((1,), (1,)), ((), ())),
            precision=lax.Precision.HIGHEST, preferred_element_type=F32,
        )
        coarse_ref[b:b + 1, :] = (scores * scale)[b:b + 1, :]

    a_copy.wait_recv()
    attention = jnp.concatenate(
        [afull[core, q] for core in range(CORES) for q in range(CHUNKS)], axis=1
    )
    width = 2 * half
    mean = jnp.sum(attention, axis=-1, keepdims=True) * (1.0 / width)
    centred = attention - mean
    variance = jnp.sum(centred * centred, axis=-1, keepdims=True) * (1.0 / width)
    normed = centred / jnp.sqrt(variance + epsilon)
    chosen_rows = xrow[...].astype(F32) + xbuf[...].astype(F32)
    mixed = (normed * gates[...] + chosen_rows).astype(BF16)
    for b in range(2):
        fine_ref[b] = dot(selt[b], mixed).astype(BF16)

    x_copy.wait_send()
    m_copy.wait_send()
    cp_copy.wait_send()
    a_copy.wait_send()

    @pl.when(holds)
    def _():
        for d in range(1, XS):
            wx_copy(d).wait_send()

    for kv in range(2):
        @pl.when(c + 2 * kv != u)
        def _():
            for copy in wf_copies(kv):
                copy.wait_send()

    for d in range(1, zs):
        qz_copy(d).wait_send()
        cz_copy(d).wait_send()
    for d in range(1, YS):
        qy_copy(d).wait_send()
        cy_copy(d).wait_send()

    def drain(q, carry):
        for d in range(1, YS):
            py_copy(q, d).wait_send()
        for d in range(1, zs):
            pz_copy(q, d).wait_send()
        return carry

    lax.fori_loop(0, CHUNKS, drain, 0)


def local(memory, contenders, wc, wm, wco, avg, idx, ext):
    users, hist, width = memory.shape
    entries = contenders.shape[1]
    half = width // 2
    zs = lax.axis_size("seq") // (CORES * YS)
    slots = YS * zs * SLOTS
    dma = pltpu.SemaphoreType.DMA
    vmem = pltpu.VMEM
    any_ = pl.BlockSpec(memory_space=pl.ANY)
    scratch = [
        vmem((users, entries, width), BF16),
        vmem((width, half), BF16),
        vmem((width, width), BF16),
        vmem((width, width), BF16),
        vmem((half, half), BF16),
        vmem((CORES, users, hist, width), BF16),
        vmem((CHUNKS, 2, width, LANES), BF16),
        vmem((2 * SLOTS, width), BF16),
        vmem((2 * SLOTS, width), BF16),
        vmem((2 * SLOTS, width), F32),
        vmem((users, 2 * SLOTS, entries), BF16),
        vmem((users, entries, 2 * SLOTS), BF16),
        vmem((YS, zs, 2 * SLOTS, half), BF16),
        vmem((users, slots, half), BF16),
        vmem((users, CORES * hist, LANES), BF16),
        vmem((users, CORES * hist, LANES), BF16),
        vmem((YS, zs, 2 * SLOTS, LANES), F32),
        vmem((CHUNKS, YS, zs, 2 * SLOTS, LANES), BF16),
        vmem((CHUNKS, zs, 2 * SLOTS, LANES), F32),
        vmem((CHUNKS, YS - 1, zs, 2 * SLOTS, LANES), BF16),
        vmem((CHUNKS, 2 * SLOTS, LANES), F32),
        vmem((CHUNKS, zs, 2 * SLOTS, LANES), BF16),
        vmem((CHUNKS, zs - 1, 2 * SLOTS, LANES), BF16),
        vmem((CORES, CHUNKS, 2 * SLOTS, LANES), F32),
        vmem((users, entries, half), F32),
        vmem((2, 8, half), F32),
        vmem((YS - 1, 8, half), F32),
        vmem((zs - 1, 8, half), F32),
        vmem((2, 8, half), F32),
        dma((6,)),
        dma((CHUNKS,)),
        dma((2,)),
        dma((2,)),
        dma((XS - 1,)),
        dma((2,)),
        dma((2, 4)),
        dma((2, 4)),
        dma((zs - 1,)),
        dma((zs - 1,)),
        dma((YS - 1,)),
        dma((YS - 1,)),
        dma((YS - 1,)),
        dma((YS - 1,)),
        dma((zs - 1,)),
        dma((zs - 1,)),
        dma((2,)),
        dma((CHUNKS, YS - 1)),
        dma((CHUNKS, YS - 1)),
        dma((CHUNKS, zs - 1)),
        dma((CHUNKS, zs - 1)),
        dma((2,)),
    ]
    return pl.pallas_call(
        functools.partial(kernel, zs),
        out_shape=(
            jax.ShapeDtypeStruct((users, entries), F32),
            jax.ShapeDtypeStruct((users, entries, width), BF16),
        ),
        in_specs=[any_] * 6
        + [pl.BlockSpec(memory_space=pltpu.VMEM), pl.BlockSpec(memory_space=pltpu.SMEM)],
        out_specs=(
            pl.BlockSpec(memory_space=pltpu.VMEM),
            pl.BlockSpec(memory_space=pltpu.VMEM),
        ),
        scratch_shapes=scratch,
        compiler_params=pltpu.CompilerParams(
            collective_id=0, has_side_effects=True, vmem_limit_bytes=56 * 1024 * 1024
        ),
        cost_estimate=pl.CostEstimate(
            flops=6_500_000_000, bytes_accessed=12_000_000, transcendentals=7_000_000
        ),
    )(memory, contenders, wc, wm, wco, avg, idx, ext)


def solution(mesh):
    placed = (
        P("user", "seq", None),
        P("user", "seq", None),
        P(),
        P(None, "user"),
        P(),
        P(),
        P("user", None),
        P("user"),
    )
    return jax.shard_map(
        local,
        mesh=mesh,
        in_specs=placed,
        out_specs=(P("user", "seq"), P("user", "seq", None)),
        check_vma=False,
    )
```

time: 402 us -> 64.2 us (0.16)
  the two profiles are of different devices: /device:TPU:1 before, /device:TPU:7 now
where the time goes in v1:
time: 64.2 us; the launch traced here: 64 us
  Pallas kernels  60.3 us (94%)
  local copies, waits for them, and re-layouts  3.07 us (5%)
    pallas_call x1, Pallas kernels, local(): pl.pallas_call(functools.partial(kernel, zs), out_shape=(jax.ShapeDtypeSt...  60.3 us
    unnamed x2, local copies, waits for them, and re-layouts  3.07 us

profile of v1, /device:TPU:7, one launch (start us, length us, event | category | flops | bytes accessed | tf_op | source)
XLA Modules:
  0.0 64.0 jit_solution(7286295566265845254)
XLA Ops:
  0.6 60.3 %shard_map.95 = (f32[2,128]{1,0:T(2,128)}, bf16[2,128,1024]{2,1,0:T(8,128)(2,1)}) custom-call(bf16[2,512,1024]{2,1,0:T(8,128)(2,1)} %m_hbm.1, bf16[2,128,1024]{2,1,0:T(8,128)(2,1)} %cand_hbm.1, bf16[1024,2048]{1,0:T(8,128)(2,1)} %wc_hbm.1, bf16[1024,512]{1,0:T(8,128)(2,1)} %wm_hbm.1, bf16[1024,1024]{1,0:T(8,128)(2,1)} %wco_hbm.1, bf16[1024,512]{1,0:T(8,128)(2,1)} %avg_hbm.1, ...), custom_call_target="tpu_custom_call" | custom-call | flops 6499999744 | bytes 12000000 | tf_op jit(solution)/shard_map/pallas_call | solution.py:516
  60.9 1.2 %copy.12 = f32[2,128]{1,0:T(2,128)} copy(f32[2,128]{1,0:T(2,128)} %get-tuple-element.4) | data formatting | bytes 2048
  62.1 1.9 %copy.13 = bf16[2,128,1024]{2,1,0:T(8,128)(2,1)} copy(bf16[2,128,1024]{2,1,0:T(8,128)(2,1)} %get-tuple-element.5) | data formatting | bytes 1048576

commit v2 on v1

--- a/solution.py
+++ b/solution.py
@@ -38,12 +38,12 @@
 def kernel(
     zs,
     m_hbm, cand_hbm, wc_hbm, wm_hbm, wco_hbm, avg_hbm, idx_ref, ext_ref,
-    coarse_ref, fine_ref,
+    coarse_ref, mixed_ref, selt,
     cand, wq, wg, wco, avg, mall, wbuf,
-    xbuf, xrow, gates, sel, selt,
+    xbuf, xrow, gates, sel,
     qbuf, q2, kbuf, vbuf, pf, psend, pown, yrecv, zown, zsend, zrecv, afull,
     pre, cs, csy, csz, pool,
-    local_sem, wl_sem, m_sem, x_sem, wx_send, wx_recv, wf_send, wf_recv,
+    local_sem, wl_sem, m_sem, x_sem, wx_send, wx_recv, wh_send, wh_recv, wf_send, wf_recv,
     qz_send, qz_recv, qy_send, qy_recv,
     cy_send, cy_recv, cz_send, cz_recv, cp_sem,
     py_send, py_recv, pz_send, pz_recv, a_sem,
@@ -56,7 +56,7 @@
     chip = s // CORES
     hist = m_hbm.shape[1]
     half = wq.shape[1]
-    colour = (y + 2 * z) % CHUNKS
+    colour = (y + z) % 2
 
     def at(x_, z_, y_, c_):
         return (x_, (z_ * YS + y_) * CORES + c_)
@@ -163,16 +163,73 @@
     x_copy = remote(xrow, xbuf, x_sem.at[0], x_sem.at[1], sibling)
     x_copy.start()
 
-    def wx_copy(d):
+    m_copy = remote(m_hbm, mall.at[c], m_sem.at[0], m_sem.at[1], sibling)
+    m_copy.start()
+
+    depth = wbuf.shape[2] // 2
+
+    def part(q, kv, high):
+        return wbuf.at[q, kv, pl.ds(high * depth, depth)]
+
+    def wx_copy(j, d):
+        q = 2 * colour + j
         return remote(
-            wm_hbm.at[:, lanes(colour * LANES, LANES)], wbuf.at[colour, own_kv],
-            wx_send.at[d - 1], wx_recv.at[own_kv], xpeer(d),
+            wm_hbm.at[:, lanes(q * LANES, LANES)], wbuf.at[q, own_kv],
+            wx_send.at[j, d // 2], wx_recv.at[j, own_kv], xpeer(d),
         )
 
     @pl.when(holds)
     def _():
-        for d in (1, 3, 2):
-            wx_copy(d).start()
+        for j in range(2):
+            for d in (1, 3):
+                wx_copy(j, d).start()
+
+    def wh_copy(j, kv, high):
+        half_ = part(2 * colour + j, kv, high)
+        return remote(
+            half_, half_, wh_send.at[j, high], wh_recv.at[j, high],
+            xpeer(XS - 1 if high else 1),
+        )
+
+    def wf_copy(j, kv, high):
+        half_ = part(2 * colour + j, kv, high)
+        peer = ypeer if j == 0 else zpeer
+        return remote(
+            half_, half_, wf_send.at[j, kv, high], wf_recv.at[j, kv, high],
+            peer((YS if j == 0 else zs) - 1 if high else 1),
+        )
+
+    def near_relay(j):
+        @pl.when(jnp.logical_not(holds))
+        def _():
+            for kv in range(2):
+                block = wbuf.at[2 * colour + j, kv]
+                remote(
+                    block, block, wx_send.at[j, 0], wx_recv.at[j, kv], xpeer(1)
+                ).wait_recv()
+                behind = (c + 2 * kv + 1) % XS == u
+
+                @pl.when(behind)
+                def _():
+                    wh_copy(j, kv, 0).start()
+
+                @pl.when(jnp.logical_not(behind))
+                def _():
+                    wh_copy(j, kv, 1).start()
+
+            for kv in range(2):
+                for high in range(2):
+                    wf_copy(j, kv, high).start()
+
+    def far_relay(j):
+        @pl.when(holds)
+        def _():
+            for high in range(2):
+                half_ = part(2 * colour + j, 1 - own_kv, high)
+                remote(
+                    half_, half_, wh_send.at[j, high], wh_recv.at[j, high], xpeer(1)
+                ).wait_recv()
+                wf_copy(j, 1 - own_kv, high).start()
 
     x_copy.wait_recv()
     rows = xrow[...].astype(F32) + xbuf[...].astype(F32)
@@ -184,57 +241,68 @@
     def qz_copy(d):
         return remote(qbuf.at[y, z], qbuf.at[y, z], qz_send.at[d - 1], qz_recv.at[d - 1], zpeer(d))
 
+    def qy_copy(d, e):
+        block = qbuf.at[y, (z - d + zs) % zs]
+        return remote(block, block, qy_send.at[d, e - 1], qy_recv.at[d, e - 1], ypeer(e))
+
+    def qy_relay(d):
+        if d > 0:
+            qz_copy(d).wait_recv()
+        for e in range(1, YS):
+            qy_copy(d, e).start()
+
     for d in range(1, zs):
         qz_copy(d).start()
-    m_copy = remote(m_hbm, mall.at[c], m_sem.at[0], m_sem.at[1], sibling)
-    m_copy.start()
-
+    qy_relay(0)
+    near_relay(0)
     l_wg.wait()
     gates[...] = silu(dot(xrow2, wg[...]))
-
-    depth = wbuf.shape[2] // 2
-
-    def wf_copies(kv):
-        block = wbuf.at[colour, kv]
-        low = wbuf.at[colour, kv, pl.ds(0, depth)]
-        high = wbuf.at[colour, kv, pl.ds(depth, depth)]
-        return (
-            remote(block, block, wf_send.at[kv, 0], wf_recv.at[kv, 0], ypeer(1)),
-            remote(block, block, wf_send.at[kv, 1], wf_recv.at[kv, 1], ypeer(YS - 1)),
-            remote(low, low, wf_send.at[kv, 2], wf_recv.at[kv, 2], zpeer(1)),
-            remote(high, high, wf_send.at[kv, 3], wf_recv.at[kv, 3], zpeer(zs - 1)),
-        )
-
-    def wx_wait(kv):
-        block = wbuf.at[colour, kv]
-        remote(block, block, wx_send.at[0], wx_recv.at[kv], xpeer(1)).wait_recv()
-
-    def forward(kv):
-        @pl.when(c + 2 * kv != u)
+    qy_relay(1)
+    qy_relay(zs - 1)
+    near_relay(1)
+    for d in (2, zs - 2):
+        qy_relay(d)
+    far_relay(0)
+    for d in range(3, zs - 2):
+        qy_relay(d)
+    far_relay(1)
+
+    l_m.wait()
+    m_copy.wait_recv()
+    spot = lax.broadcasted_iota(jnp.int32, (hist, LANES), 0)
+
+    def project(q):
+        def block(i, carry):
+            b, core = i // CORES, i % CORES
+            weights = jnp.concatenate([wbuf[q, 0], wbuf[q, 1]], axis=1)
+            raw = dot(mall[core, b], weights)
+            at_rows = pl.ds(pl.multiple_of(core * hist, hist), hist)
+            kbuf[q, b, at_rows, :] = silu(raw[:, :LANES]).astype(BF16)
+            place = (chip * CORES + core) * hist + spot
+            vbuf[q, b, at_rows, :] = jnp.where(
+                place < ext_ref[b], raw[:, LANES:], 0.0
+            ).astype(BF16)
+            return carry
+
+        lax.fori_loop(0, 2 * CORES, block, 0)
+
+    def own_chunk(j, carry):
+        q = 2 * colour + j
+
+        @pl.when(holds)
         def _():
-            wx_wait(kv)
-            for copy in wf_copies(kv):
-                copy.start()
-
-    forward(0)
-    forward(1)
-
-    for d in range(1, zs):
-        qz_copy(d).wait_recv()
-
-    def qy_copy(d):
-        return remote(qbuf.at[y], qbuf.at[y], qy_send.at[d - 1], qy_recv.at[d - 1], ypeer(d))
-
-    for d in range(1, YS):
-        qy_copy(d).start()
+            wl_copy(q).wait()
+
+        project(q)
+        return carry
+
+    lax.fori_loop(0, 2, own_chunk, 0)
 
     l_wco.wait()
     for b in range(2):
         hidden = dot(cand[b], wco[...])
         pre[b] = silu(hidden[:, :half]) * hidden[:, half:]
 
-    l_m.wait()
-    m_copy.wait_recv()
     live_row = lax.broadcasted_iota(jnp.int32, (rows16, hist), 0)
     live_col = lax.broadcasted_iota(jnp.int32, (rows16, hist), 1)
     total = jnp.zeros((rows16, half), F32)
@@ -243,7 +311,9 @@
             place = (chip * CORES + core) * hist + live_col
             mask = jnp.where((live_row == b) & (place < ext_ref[b]), 1.0, 0.0).astype(BF16)
             total = total + dot(mask, mall[core, b, :, lanes(c * half, half)])
-    cs[0] = total[:8]
+    cs[0] = jnp.concatenate(
+        [total[:2, i * LANES:(i + 1) * LANES] for i in range(half // LANES)], axis=0
+    )
 
     def cy_copy(d):
         return remote(cs.at[0], csy.at[d - 1], cy_send.at[d - 1], cy_recv.at[d - 1], ypeer(d))
@@ -254,13 +324,31 @@
     for d in range(1, YS):
         cy_copy(d).start()
 
-    for d in range(1, YS):
-        qy_copy(d).wait_recv()
+    for j in range(2):
+        other = 2 * (1 - colour) + j
+        for kv in range(2):
+            @pl.when(c + 2 * kv == u)
+            def _():
+                wl_copy(other).wait()
+
+            @pl.when(c + 2 * kv != u)
+            def _():
+                for high in range(2):
+                    half_ = part(other, kv, high)
+                    remote(
+                        half_, half_, wf_send.at[j, kv, high], wf_recv.at[j, kv, high], ypeer(1)
+                    ).wait_recv()
+
+        project(other)
+
+    for d in range(zs):
+        for e in range(1, YS):
+            qy_copy(d, e).wait_recv()
     for yy in range(YS):
         block = qbuf[yy].astype(F32)
         for b in range(2):
-            part = block[:, b * SLOTS:(b + 1) * SLOTS, :].reshape(zs * SLOTS, half)
-            q2[b, yy * zs * SLOTS:(yy + 1) * zs * SLOTS, :] = part.astype(BF16)
+            own_rows = block[:, b * SLOTS:(b + 1) * SLOTS, :].reshape(zs * SLOTS, half)
+            q2[b, yy * zs * SLOTS:(yy + 1) * zs * SLOTS, :] = own_rows.astype(BF16)
 
     for d in range(1, YS):
         cy_copy(d).wait_recv()
@@ -282,58 +370,17 @@
 
     lane = lax.broadcasted_iota(jnp.int32, (YS * zs * SLOTS, LANES), 1)
     first = lane < (LANES // 2)
-    spot = lax.broadcasted_iota(jnp.int32, (hist, LANES), 0)
-
-    def w_wait(q, kv):
-        near = (q - colour + CHUNKS) % CHUNKS
-        local_ = c + 2 * kv == u
-
-        @pl.when(local_)
-        def _():
-            wl_copy(q).wait()
-
-        @pl.when(jnp.logical_not(local_))
-        def _():
-            copies = wf_copies(kv)
-
-            @pl.when(near == 1)
-            def _():
-                copies[1].wait_recv()
-
-            @pl.when(near == 3)
-            def _():
-                copies[0].wait_recv()
-
-            @pl.when(near == 2)
-            def _():
-                copies[2].wait_recv()
-                copies[3].wait_recv()
 
     def compute(q):
-        w_wait(q, 0)
-        w_wait(q, 1)
-
-        def project(i, carry):
-            b, core = i // CORES, i % CORES
-            weights = jnp.concatenate([wbuf[q, 0], wbuf[q, 1]], axis=1)
-            raw = dot(mall[core, b], weights)
-            at_rows = pl.ds(pl.multiple_of(core * hist, hist), hist)
-            kbuf[b, at_rows, :] = silu(raw[:, :LANES]).astype(BF16)
-            place = (chip * CORES + core) * hist + spot
-            vbuf[b, at_rows, :] = jnp.where(place < ext_ref[b], raw[:, LANES:], 0.0).astype(BF16)
-            return carry
-
-        lax.fori_loop(0, 2 * CORES, project, 0)
-
         for b in range(2):
             queries_ = q2[b, :, lanes(q * LANES, LANES)]
             outs = []
             for h in range(2):
                 keep = first if h == 0 else jnp.logical_not(first)
                 masked = jnp.where(keep, queries_.astype(F32), 0.0).astype(BF16)
-                logits = dot_nt(masked, kbuf[b])
+                logits = dot_nt(masked, kbuf[q, b])
                 weights = (logits + logits * jnp.tanh(logits)).astype(BF16)
-                outs.append(dot(weights, vbuf[b]))
+                outs.append(dot(weights, vbuf[q, b]))
             out = jnp.where(first, outs[0], outs[1])
             pf[:, :, b * SLOTS:(b + 1) * SLOTS, :] = out.reshape(YS, zs, SLOTS, LANES)
         psend[q] = pf[...].astype(BF16)
@@ -368,9 +415,13 @@
 
     for d in range(1, zs):
         cz_copy(d).wait_recv()
-    summed = cs[1]
+    packed = cs[1]
     for d in range(1, zs):
-        summed = summed + csz[d - 1]
+        packed = packed + csz[d - 1]
+    summed = jnp.concatenate(
+        [packed[2 * i:2 * i + 2] for i in range(half // LANES)], axis=1
+    )
+    summed = jnp.concatenate([summed, jnp.zeros((6, half), F32)], axis=0)
     l_avg.wait()
     part1 = summed.astype(BF16)
     rest = summed - part1.astype(F32)
@@ -414,9 +465,7 @@
     variance = jnp.sum(centred * centred, axis=-1, keepdims=True) * (1.0 / width)
     normed = centred / jnp.sqrt(variance + epsilon)
     chosen_rows = xrow[...].astype(F32) + xbuf[...].astype(F32)
-    mixed = (normed * gates[...] + chosen_rows).astype(BF16)
-    for b in range(2):
-        fine_ref[b] = dot(selt[b], mixed).astype(BF16)
+    mixed_ref[...] = (normed * gates[...] + chosen_rows).astype(BF16)
 
     x_copy.wait_send()
     m_copy.wait_send()
@@ -425,21 +474,28 @@
 
     @pl.when(holds)
     def _():
-        for d in range(1, XS):
-            wx_copy(d).wait_send()
-
-    for kv in range(2):
-        @pl.when(c + 2 * kv != u)
-        def _():
-            for copy in wf_copies(kv):
-                copy.wait_send()
+        for j in range(2):
+            for d in (1, 3):
+                wx_copy(j, d).wait_send()
+            for high in range(2):
+                wf_copy(j, 1 - own_kv, high).wait_send()
+
+    @pl.when(jnp.logical_not(holds))
+    def _():
+        for j in range(2):
+            for high in range(2):
+                wh_copy(j, 0, high).wait_send()
+                for kv in range(2):
+                    wf_copy(j, kv, high).wait_send()
 
     for d in range(1, zs):
         qz_copy(d).wait_send()
         cz_copy(d).wait_send()
     for d in range(1, YS):
-        qy_copy(d).wait_send()
         cy_copy(d).wait_send()
+    for d in range(zs):
+        for e in range(1, YS):
+            qy_copy(d, e).wait_send()
 
     def drain(q, carry):
         for d in range(1, YS):
@@ -449,6 +505,12 @@
         return carry
 
     lax.fori_loop(0, CHUNKS, drain, 0)
+
+
+def place_kernel(scores_ref, mixed_ref, selt_ref, coarse_ref, fine_ref):
+    coarse_ref[...] = scores_ref[...]
+    for b in range(fine_ref.shape[0]):
+        fine_ref[b] = dot(selt_ref[b], mixed_ref[...]).astype(BF16)
 
 
 def local(memory, contenders, wc, wm, wco, avg, idx, ext):
@@ -472,11 +534,10 @@
         vmem((2 * SLOTS, width), BF16),
         vmem((2 * SLOTS, width), F32),
         vmem((users, 2 * SLOTS, entries), BF16),
-        vmem((users, entries, 2 * SLOTS), BF16),
         vmem((YS, zs, 2 * SLOTS, half), BF16),
         vmem((users, slots, half), BF16),
-        vmem((users, CORES * hist, LANES), BF16),
-        vmem((users, CORES * hist, LANES), BF16),
+        vmem((CHUNKS, users, CORES * hist, LANES), BF16),
+        vmem((CHUNKS, users, CORES * hist, LANES), BF16),
         vmem((YS, zs, 2 * SLOTS, LANES), F32),
         vmem((CHUNKS, YS, zs, 2 * SLOTS, LANES), BF16),
         vmem((CHUNKS, zs, 2 * SLOTS, LANES), F32),
@@ -486,22 +547,24 @@
         vmem((CHUNKS, zs - 1, 2 * SLOTS, LANES), BF16),
         vmem((CORES, CHUNKS, 2 * SLOTS, LANES), F32),
         vmem((users, entries, half), F32),
-        vmem((2, 8, half), F32),
-        vmem((YS - 1, 8, half), F32),
-        vmem((zs - 1, 8, half), F32),
+        vmem((2, 8, LANES), F32),
+        vmem((YS - 1, 8, LANES), F32),
+        vmem((zs - 1, 8, LANES), F32),
         vmem((2, 8, half), F32),
         dma((6,)),
         dma((CHUNKS,)),
         dma((2,)),
         dma((2,)),
-        dma((XS - 1,)),
-        dma((2,)),
-        dma((2, 4)),
-        dma((2, 4)),
+        dma((2, 2)),
+        dma((2, 2)),
+        dma((2, 2)),
+        dma((2, 2)),
+        dma((2, 2, 2)),
+        dma((2, 2, 2)),
         dma((zs - 1,)),
         dma((zs - 1,)),
-        dma((YS - 1,)),
-        dma((YS - 1,)),
+        dma((zs, YS - 1)),
+        dma((zs, YS - 1)),
         dma((YS - 1,)),
         dma((YS - 1,)),
         dma((zs - 1,)),
@@ -513,18 +576,17 @@
         dma((CHUNKS, zs - 1)),
         dma((2,)),
     ]
-    return pl.pallas_call(
+    vm = pl.BlockSpec(memory_space=pltpu.VMEM)
+    scores, mixed, selt = pl.pallas_call(
         functools.partial(kernel, zs),
         out_shape=(
             jax.ShapeDtypeStruct((users, entries), F32),
-            jax.ShapeDtypeStruct((users, entries, width), BF16),
+            jax.ShapeDtypeStruct((2 * SLOTS, width), BF16),
+            jax.ShapeDtypeStruct((users, entries, 2 * SLOTS), BF16),
         ),
         in_specs=[any_] * 6
         + [pl.BlockSpec(memory_space=pltpu.VMEM), pl.BlockSpec(memory_space=pltpu.SMEM)],
-        out_specs=(
-            pl.BlockSpec(memory_space=pltpu.VMEM),
-            pl.BlockSpec(memory_space=pltpu.VMEM),
-        ),
+        out_specs=(vm, vm, vm),
         scratch_shapes=scratch,
         compiler_params=pltpu.CompilerParams(
             collective_id=0, has_side_effects=True, vmem_limit_bytes=56 * 1024 * 1024
@@ -533,6 +595,15 @@
             flops=6_500_000_000, bytes_accessed=12_000_000, transcendentals=7_000_000
         ),
     )(memory, contenders, wc, wm, wco, avg, idx, ext)
+    return pl.pallas_call(
+        place_kernel,
+        out_shape=(
+            jax.ShapeDtypeStruct((users, entries), F32),
+            jax.ShapeDtypeStruct((users, entries, width), BF16),
+        ),
+        in_specs=[vm, vm, vm],
+        out_specs=(vm, vm),
+    )(scores, mixed, selt)
 
 
 def solution(mesh):

time: 64.2 us -> 58.1 us (0.905)
  the two profiles are of different devices: /device:TPU:7 before, /device:TPU:1 now
where the time goes in v2:
time: 58.1 us; the launch traced here: 57.9 us
  Pallas kernels  57.3 us (99%)
  between operations  0.64 us (1%)
    pallas_call x1, Pallas kernels, local(): pl.pallas_call(functools.partial(kernel, zs), out_shape=(jax.ShapeDtypeSt...  55.4 us
    pallas_call x1, Pallas kernels, local(): pl.pallas_call(place_kernel, out_shape=(jax.ShapeDtypeStruct((users, entr...  1.92 us

profile of v2, /device:TPU:1, one launch (start us, length us, event | category | flops | bytes accessed | tf_op | source)
XLA Modules:
  0.0 57.9 jit_solution(5380860217010778643)
XLA Ops:
  0.6 55.4 %shard_map.95 = (f32[2,128]{1,0:T(2,128)}, bf16[16,1024]{1,0:T(8,128)(2,1)}, bf16[2,128,16]{2,1,0:T(8,128)(2,1)}) custom-call(bf16[2,512,1024]{2,1,0:T(8,128)(2,1)} %m_hbm.1, bf16[2,128,1024]{2,1,0:T(8,128)(2,1)} %cand_hbm.1, bf16[1024,2048]{1,0:T(8,128)(2,1)} %wc_hbm.1, bf16[1024,512]{1,0:T(8,128)(2,1)} %wm_hbm.1, bf16[1024,1024]{1,0:T(8,128)(2,1)} %wco_hbm.1, ...), custom_call_target="tpu_custom_call" | custom-call | flops 6499999744 | bytes 12000000 | tf_op jit(solution)/shard_map/pallas_call | solution.py:580
  56.0 1.9 %shard_map.96 = (f32[2,128]{1,0:T(2,128)}, bf16[2,128,1024]{2,1,0:T(8,128)(2,1)}) custom-call(f32[2,128]{1,0:T(2,128)} %get-tuple-element.5.scores_ref, bf16[16,1024]{1,0:T(8,128)(2,1)} %get-tuple-element.6.mixed_ref, bf16[2,128,16]{2,1,0:T(8,128)(2,1)} %get-tuple-element.7.selt_ref), custom_call_target="tpu_custom_call" | custom-call | tf_op jit(solution)/shard_map/pallas_call | solution.py:598

commit v3 on v2

--- a/solution.py
+++ b/solution.py
@@ -46,7 +46,7 @@
     local_sem, wl_sem, m_sem, x_sem, wx_send, wx_recv, wh_send, wh_recv, wf_send, wf_recv,
     qz_send, qz_recv, qy_send, qy_recv,
     cy_send, cy_recv, cz_send, cz_recv, cp_sem,
-    py_send, py_recv, pz_send, pz_recv, a_sem,
+    py_send, py_recv, pz_send, pz_recv, a_sem, far_sem,
 ):
     u = lax.axis_index("user")
     s = lax.axis_index("seq")
@@ -85,7 +85,7 @@
     l_wq = pltpu.make_async_copy(
         wc_hbm.at[:, lanes(2 * half + c * half, half)], wq, local_sem.at[1]
     )
-    l_m = pltpu.make_async_copy(m_hbm, mall.at[c], local_sem.at[2])
+    l_m = pltpu.make_async_copy(m_hbm, mall.at[:, c], local_sem.at[2])
     l_wg = pltpu.make_async_copy(wc_hbm.at[:, pl.ds(0, 2 * half)], wg, local_sem.at[3])
     l_wco = pltpu.make_async_copy(wco_hbm, wco, local_sem.at[4])
     l_avg = pltpu.make_async_copy(
@@ -94,36 +94,33 @@
     l_cand.start()
     l_wq.start()
 
+    own_kv = u // 2
+    holds = (u % 2) == c
+
+    def wl_copy(q):
+        return pltpu.make_async_copy(
+            wm_hbm.at[:, lanes(q * LANES, LANES)], wbuf.at[q, own_kv], wl_sem.at[q]
+        )
+
+    @pl.when(holds)
+    def _():
+        for i in range(CHUNKS):
+            wl_copy((2 * colour + i) % CHUNKS).start()
+
     barrier = pltpu.get_barrier_semaphore()
 
     def greet(device):
         pl.semaphore_signal(barrier, inc=1, device_id=device, device_id_type=MESH)
 
     greet(sibling)
-    for d in range(1, XS):
-        greet(xpeer(d))
-    for d in range(1, YS):
-        greet(ypeer(d))
-    for d in range(1, zs):
-        greet(zpeer(d))
+    for peer, size in ((xpeer, XS), (ypeer, YS), (zpeer, zs)):
+        greet(peer(1))
+        greet(peer(size - 1))
 
     l_m.start()
     l_wg.start()
     l_wco.start()
     l_avg.start()
-
-    own_kv = u // 2
-    holds = (u % 2) == c
-
-    def wl_copy(q):
-        return pltpu.make_async_copy(
-            wm_hbm.at[:, lanes(q * LANES, LANES)], wbuf.at[q, own_kv], wl_sem.at[q]
-        )
-
-    @pl.when(holds)
-    def _():
-        for q in range(CHUNKS):
-            wl_copy(q).start()
 
     rows16 = 2 * SLOTS
     ones = jnp.ones((rows16, idx_ref.shape[1]), BF16)
@@ -158,68 +155,78 @@
     found = dot(sel[0], cand[0]) + dot(sel[1], cand[1])
     xrow[...] = found.astype(BF16)
 
-    pl.semaphore_wait(barrier, 1 + (XS - 1) + (YS - 1) + (zs - 1))
+    pl.semaphore_wait(barrier, 7)
+
+    def tell(r, peer, size):
+        for side, d in ((0, 1), (1, size - 1)):
+            pl.semaphore_signal(
+                far_sem.at[r, side], inc=1, device_id=peer(d), device_id_type=MESH
+            )
+
+    def hear(r):
+        for side in range(2):
+            pl.semaphore_wait(far_sem.at[r, side], 1)
+
+    rounds = zs // 2 - 1
+    tell(0, zpeer, zs)
+    tell(rounds, ypeer, YS)
 
     x_copy = remote(xrow, xbuf, x_sem.at[0], x_sem.at[1], sibling)
     x_copy.start()
 
-    m_copy = remote(m_hbm, mall.at[c], m_sem.at[0], m_sem.at[1], sibling)
+    m_copy = remote(m_hbm, mall.at[:, c], m_sem.at[0], m_sem.at[1], sibling)
     m_copy.start()
 
     depth = wbuf.shape[2] // 2
 
     def part(q, kv, high):
-        return wbuf.at[q, kv, pl.ds(high * depth, depth)]
-
-    def wx_copy(j, d):
-        q = 2 * colour + j
+        return wbuf.at[q, kv, pl.ds(pl.multiple_of(high * depth, depth), depth)]
+
+    def wx_copy(j, high, d):
+        half_ = part(2 * colour + j, own_kv, high)
         return remote(
-            wm_hbm.at[:, lanes(q * LANES, LANES)], wbuf.at[q, own_kv],
-            wx_send.at[j, d // 2], wx_recv.at[j, own_kv], xpeer(d),
+            half_, half_, wx_send.at[j, high, d // 2], wx_recv.at[j, high, own_kv], xpeer(d)
         )
 
     @pl.when(holds)
     def _():
-        for j in range(2):
-            for d in (1, 3):
-                wx_copy(j, d).start()
+        for i in range(2):
+            for j in range(2):
+                if i == 0:
+                    wl_copy(2 * colour + j).wait()
+                wx_copy(j, i, 1).start()
+                wx_copy(j, 1 - i, XS - 1).start()
 
     def wh_copy(j, kv, high):
         half_ = part(2 * colour + j, kv, high)
         return remote(
             half_, half_, wh_send.at[j, high], wh_recv.at[j, high],
-            xpeer(XS - 1 if high else 1),
+            xpeer(1 + high * (XS - 2)),
         )
 
     def wf_copy(j, kv, high):
         half_ = part(2 * colour + j, kv, high)
-        peer = ypeer if j == 0 else zpeer
+        if j == 0:
+            device = ypeer(1 + high * (YS - 2))
+        else:
+            device = zpeer(1 + high * (zs - 2))
         return remote(
-            half_, half_, wf_send.at[j, kv, high], wf_recv.at[j, kv, high],
-            peer((YS if j == 0 else zs) - 1 if high else 1),
-        )
-
-    def near_relay(j):
+            half_, half_, wf_send.at[j, kv, high], wf_recv.at[j, kv, high], device
+        )
+
+    def near_relay(i, j):
         @pl.when(jnp.logical_not(holds))
         def _():
             for kv in range(2):
-                block = wbuf.at[2 * colour + j, kv]
+                behind = (c + 2 * kv + 1) % XS == u
+                high = jnp.where(behind, i, 1 - i)
+                half_ = part(2 * colour + j, kv, high)
                 remote(
-                    block, block, wx_send.at[j, 0], wx_recv.at[j, kv], xpeer(1)
+                    half_, half_, wx_send.at[j, high, 0], wx_recv.at[j, high, kv], xpeer(1)
                 ).wait_recv()
-                behind = (c + 2 * kv + 1) % XS == u
-
-                @pl.when(behind)
-                def _():
-                    wh_copy(j, kv, 0).start()
-
-                @pl.when(jnp.logical_not(behind))
-                def _():
-                    wh_copy(j, kv, 1).start()
-
-            for kv in range(2):
-                for high in range(2):
-                    wf_copy(j, kv, high).start()
+                if i == 0:
+                    wh_copy(j, kv, high).start()
+                wf_copy(j, kv, high).start()
 
     def far_relay(j):
         @pl.when(holds)
@@ -234,6 +241,8 @@
     x_copy.wait_recv()
     rows = xrow[...].astype(F32) + xbuf[...].astype(F32)
     xrow2 = rows.astype(BF16)
+    hear(0)
+    tell(1, zpeer, zs)
     l_wq.wait()
     queries = silu(dot(xrow2, wq[...])).astype(BF16)
     qbuf[y, z] = (queries.astype(F32) * (0.5 / math.sqrt(2 * half // HEADS))).astype(BF16)
@@ -251,49 +260,48 @@
         for e in range(1, YS):
             qy_copy(d, e).start()
 
-    for d in range(1, zs):
+    for d in (1, zs - 1, 2, zs - 2):
         qz_copy(d).start()
+    near_relay(0, 0)
+    for r in range(1, rounds):
+        hear(r)
+        if r + 1 < rounds:
+            tell(r + 1, zpeer, zs)
+        for d in sorted({r + 2, zs - r - 2}):
+            qz_copy(d).start()
+    hear(rounds)
     qy_relay(0)
-    near_relay(0)
+    near_relay(0, 1)
     l_wg.wait()
     gates[...] = silu(dot(xrow2, wg[...]))
     qy_relay(1)
     qy_relay(zs - 1)
-    near_relay(1)
+    near_relay(1, 0)
+    far_relay(0)
+    near_relay(1, 1)
     for d in (2, zs - 2):
         qy_relay(d)
-    far_relay(0)
+    far_relay(1)
     for d in range(3, zs - 2):
         qy_relay(d)
-    far_relay(1)
 
     l_m.wait()
     m_copy.wait_recv()
-    spot = lax.broadcasted_iota(jnp.int32, (hist, LANES), 0)
+    both = CORES * hist
+    spot = chip * both + lax.broadcasted_iota(jnp.int32, (both, LANES), 0)
 
     def project(q):
-        def block(i, carry):
-            b, core = i // CORES, i % CORES
+        def block(b, carry):
             weights = jnp.concatenate([wbuf[q, 0], wbuf[q, 1]], axis=1)
-            raw = dot(mall[core, b], weights)
-            at_rows = pl.ds(pl.multiple_of(core * hist, hist), hist)
-            kbuf[q, b, at_rows, :] = silu(raw[:, :LANES]).astype(BF16)
-            place = (chip * CORES + core) * hist + spot
-            vbuf[q, b, at_rows, :] = jnp.where(
-                place < ext_ref[b], raw[:, LANES:], 0.0
-            ).astype(BF16)
+            raw = dot(mall[b].reshape(both, 2 * half), weights)
+            kbuf[q, b] = silu(raw[:, :LANES]).astype(BF16)
+            vbuf[q, b] = jnp.where(spot < ext_ref[b], raw[:, LANES:], 0.0).astype(BF16)
             return carry
 
-        lax.fori_loop(0, 2 * CORES, block, 0)
+        lax.fori_loop(0, 2, block, 0)
 
     def own_chunk(j, carry):
-        q = 2 * colour + j
-
-        @pl.when(holds)
-        def _():
-            wl_copy(q).wait()
-
-        project(q)
+        project(2 * colour + j)
         return carry
 
     lax.fori_loop(0, 2, own_chunk, 0)
@@ -310,7 +318,7 @@
         for core in range(CORES):
             place = (chip * CORES + core) * hist + live_col
             mask = jnp.where((live_row == b) & (place < ext_ref[b]), 1.0, 0.0).astype(BF16)
-            total = total + dot(mask, mall[core, b, :, lanes(c * half, half)])
+            total = total + dot(mask, mall[b, core, :, lanes(c * half, half)])
     cs[0] = jnp.concatenate(
         [total[:2, i * LANES:(i + 1) * LANES] for i in range(half // LANES)], axis=0
     )
@@ -475,9 +483,9 @@
     @pl.when(holds)
     def _():
         for j in range(2):
-            for d in (1, 3):
-                wx_copy(j, d).wait_send()
             for high in range(2):
+                wx_copy(j, high, 1).wait_send()
+                wx_copy(j, high, XS - 1).wait_send()
                 wf_copy(j, 1 - own_kv, high).wait_send()
 
     @pl.when(jnp.logical_not(holds))
@@ -528,7 +536,7 @@
         vmem((width, width), BF16),
         vmem((width, width), BF16),
         vmem((half, half), BF16),
-        vmem((CORES, users, hist, width), BF16),
+        vmem((users, CORES, hist, width), BF16),
         vmem((CHUNKS, 2, width, LANES), BF16),
         vmem((2 * SLOTS, width), BF16),
         vmem((2 * SLOTS, width), BF16),
@@ -555,8 +563,8 @@
         dma((CHUNKS,)),
         dma((2,)),
         dma((2,)),
-        dma((2, 2)),
-        dma((2, 2)),
+        dma((2, 2, 2)),
+        dma((2, 2, 2)),
         dma((2, 2)),
         dma((2, 2)),
         dma((2, 2, 2)),
@@ -575,6 +583,7 @@
         dma((CHUNKS, zs - 1)),
         dma((CHUNKS, zs - 1)),
         dma((2,)),
+        pltpu.SemaphoreType.REGULAR((zs // 2, 2)),
     ]
     vm = pl.BlockSpec(memory_space=pltpu.VMEM)
     scores, mixed, selt = pl.pallas_call(

time: 58.1 us -> 54.3 us (0.935)
  Pallas kernels: 57.3 us -> 53.5 us
    pallas_call x1, Pallas kernels: 55.4 us -> 51.6 us  [local(): pl.pallas_call(functools.partial(kernel, zs), out_shape=(jax.ShapeDtypeSt...]
where the time goes in v3:
time: 54.3 us; the launch traced here: 54.1 us
  Pallas kernels  53.5 us (99%)
  between operations  0.64 us (1%)
    pallas_call x1, Pallas kernels, local(): pl.pallas_call(functools.partial(kernel, zs), out_shape=(jax.ShapeDtypeSt...  51.6 us
    pallas_call x1, Pallas kernels, local(): pl.pallas_call(place_kernel, out_shape=(jax.ShapeDtypeStruct((users, entr...  1.92 us

profile of v3, /device:TPU:1, one launch (start us, length us, event | category | flops | bytes accessed | tf_op | source)
XLA Modules:
  0.0 54.1 jit_solution(1522419432532512501)
XLA Ops:
  0.6 51.6 %shard_map.95 = (f32[2,128]{1,0:T(2,128)}, bf16[16,1024]{1,0:T(8,128)(2,1)}, bf16[2,128,16]{2,1,0:T(8,128)(2,1)}) custom-call(bf16[2,512,1024]{2,1,0:T(8,128)(2,1)} %m_hbm.1, bf16[2,128,1024]{2,1,0:T(8,128)(2,1)} %cand_hbm.1, bf16[1024,2048]{1,0:T(8,128)(2,1)} %wc_hbm.1, bf16[1024,512]{1,0:T(8,128)(2,1)} %wm_hbm.1, bf16[1024,1024]{1,0:T(8,128)(2,1)} %wco_hbm.1, ...), custom_call_target="tpu_custom_call" | custom-call | flops 6499999744 | bytes 12000000 | tf_op jit(solution)/shard_map/pallas_call | solution.py:589
  52.2 1.9 %shard_map.96 = (f32[2,128]{1,0:T(2,128)}, bf16[2,128,1024]{2,1,0:T(8,128)(2,1)}) custom-call(f32[2,128]{1,0:T(2,128)} %get-tuple-element.5.scores_ref, bf16[16,1024]{1,0:T(8,128)(2,1)} %get-tuple-element.6.mixed_ref, bf16[2,128,16]{2,1,0:T(8,128)(2,1)} %get-tuple-element.7.selt_ref), custom_call_target="tpu_custom_call" | custom-call | tf_op jit(solution)/shard_map/pallas_call | solution.py:607

commit v4 on v3

--- a/solution.py
+++ b/solution.py
@@ -80,6 +80,9 @@
             src_ref=src, dst_ref=dst, send_sem=send, recv_sem=recv,
             device_id=device, device_id_type=MESH,
         )
+
+    def settle(ref, sem):
+        pltpu.make_async_copy(ref, ref, sem).wait()
 
     l_cand = pltpu.make_async_copy(cand_hbm, cand, local_sem.at[0])
     l_wq = pltpu.make_async_copy(
@@ -252,7 +255,7 @@
 
     def qy_copy(d, e):
         block = qbuf.at[y, (z - d + zs) % zs]
-        return remote(block, block, qy_send.at[d, e - 1], qy_recv.at[d, e - 1], ypeer(e))
+        return remote(block, block, qy_send.at[0], qy_recv.at[0], ypeer(e))
 
     def qy_relay(d):
         if d > 0:
@@ -324,10 +327,10 @@
     )
 
     def cy_copy(d):
-        return remote(cs.at[0], csy.at[d - 1], cy_send.at[d - 1], cy_recv.at[d - 1], ypeer(d))
+        return remote(cs.at[0], csy.at[d - 1], cy_send.at[0], cy_recv.at[0], ypeer(d))
 
     def cz_copy(d):
-        return remote(cs.at[1], csz.at[d - 1], cz_send.at[d - 1], cz_recv.at[d - 1], zpeer(d))
+        return remote(cs.at[1], csz.at[d - 1], cz_send.at[0], cz_recv.at[0], zpeer(d))
 
     for d in range(1, YS):
         cy_copy(d).start()
@@ -349,17 +352,15 @@
 
         project(other)
 
-    for d in range(zs):
-        for e in range(1, YS):
-            qy_copy(d, e).wait_recv()
+    others = qbuf.at[pl.ds(0, YS - 1)]
+    settle(others, qy_recv.at[0])
     for yy in range(YS):
         block = qbuf[yy].astype(F32)
         for b in range(2):
             own_rows = block[:, b * SLOTS:(b + 1) * SLOTS, :].reshape(zs * SLOTS, half)
             q2[b, yy * zs * SLOTS:(yy + 1) * zs * SLOTS, :] = own_rows.astype(BF16)
 
-    for d in range(1, YS):
-        cy_copy(d).wait_recv()
+    settle(csy, cy_recv.at[0])
     cs[1] = cs[0] + (csy[0] + csy[1] + csy[2])
     for d in range(1, zs):
         cz_copy(d).start()
@@ -367,13 +368,13 @@
     def py_copy(q, d):
         return remote(
             psend.at[q, (y + d) % YS], yrecv.at[q, d - 1],
-            py_send.at[q, d - 1], py_recv.at[q, d - 1], ypeer(d),
+            py_send.at[q], py_recv.at[q], ypeer(d),
         )
 
     def pz_copy(q, d):
         return remote(
             zsend.at[q, (z + d) % zs], zrecv.at[q, d - 1],
-            pz_send.at[q, d - 1], pz_recv.at[q, d - 1], zpeer(d),
+            pz_send.at[q], pz_recv.at[q], zpeer(d),
         )
 
     lane = lax.broadcasted_iota(jnp.int32, (YS * zs * SLOTS, LANES), 1)
@@ -382,14 +383,15 @@
     def compute(q):
         for b in range(2):
             queries_ = q2[b, :, lanes(q * LANES, LANES)]
-            outs = []
-            for h in range(2):
-                keep = first if h == 0 else jnp.logical_not(first)
-                masked = jnp.where(keep, queries_.astype(F32), 0.0).astype(BF16)
-                logits = dot_nt(masked, kbuf[q, b])
-                weights = (logits + logits * jnp.tanh(logits)).astype(BF16)
-                outs.append(dot(weights, vbuf[q, b]))
-            out = jnp.where(first, outs[0], outs[1])
+            wide = queries_.astype(F32)
+            masked = jnp.concatenate(
+                [jnp.where(first, wide, 0.0), jnp.where(first, 0.0, wide)], axis=0
+            ).astype(BF16)
+            logits = dot_nt(masked, kbuf[q, b])
+            weights = (logits + logits * jnp.tanh(logits)).astype(BF16)
+            outs = dot(weights, vbuf[q, b])
+            count = YS * zs * SLOTS
+            out = jnp.where(first, outs[:count], outs[count:])
             pf[:, :, b * SLOTS:(b + 1) * SLOTS, :] = out.reshape(YS, zs, SLOTS, LANES)
         psend[q] = pf[...].astype(BF16)
         pown[q] = pf[y]
@@ -397,8 +399,7 @@
             py_copy(q, d).start()
 
     def reduce_y(q):
-        for d in range(1, YS):
-            py_copy(q, d).wait_recv()
+        settle(yrecv.at[q], py_recv.at[q])
         total_ = pown[q]
         for d in range(1, YS):
             total_ = total_ + yrecv[q, d - 1].astype(F32)
@@ -409,20 +410,36 @@
             pz_copy(q, d).start()
 
     def step(q, carry):
-        @pl.when(q < CHUNKS)
-        def _():
-            compute(q)
-
-        @pl.when(q > 0)
-        def _():
-            reduce_y(q - 1)
-
+        compute(q)
         return carry
 
-    lax.fori_loop(0, CHUNKS + 1, step, 0)
+    lax.fori_loop(0, CHUNKS, step, 0)
+
+    x_copy.wait_send()
+    m_copy.wait_send()
+
+    @pl.when(holds)
+    def _():
+        for j in range(2):
+            for high in range(2):
+                wx_copy(j, high, 1).wait_send()
+                wx_copy(j, high, XS - 1).wait_send()
+                wf_copy(j, 1 - own_kv, high).wait_send()
+
+    @pl.when(jnp.logical_not(holds))
+    def _():
+        for j in range(2):
+            for high in range(2):
+                wh_copy(j, 0, high).wait_send()
+                for kv in range(2):
+                    wf_copy(j, kv, high).wait_send()
 
     for d in range(1, zs):
-        cz_copy(d).wait_recv()
+        qz_copy(d).wait_send()
+    settle(others, qy_send.at[0])
+    settle(csy, cy_send.at[0])
+
+    settle(csz, cz_recv.at[0])
     packed = cs[1]
     for d in range(1, zs):
         packed = packed + csz[d - 1]
@@ -439,10 +456,23 @@
     cp_copy = remote(pool.at[0], pool.at[1], cp_sem.at[0], cp_sem.at[1], sibling)
     cp_copy.start()
 
+    def after(q, carry):
+        reduce_y(q)
+        return carry
+
+    lax.fori_loop(0, CHUNKS, after, 0)
+
+    def drain(q, carry):
+        settle(yrecv.at[q], py_send.at[q])
+        return carry
+
+    lax.fori_loop(0, CHUNKS, drain, 0)
+    settle(csz, cz_send.at[0])
+
     def reduce_z(q, carry):
         total_ = zown[q]
+        settle(zrecv.at[q], pz_recv.at[q])
         for d in range(1, zs):
-            pz_copy(q, d).wait_recv()
             total_ = total_ + zrecv[q, d - 1].astype(F32)
         afull[c, q] = total_
         return carry
@@ -451,7 +481,13 @@
     a_copy = remote(afull.at[c], afull.at[c], a_sem.at[0], a_sem.at[1], sibling)
     a_copy.start()
 
-    cp_copy.wait_recv()
+    def drain_z(q, carry):
+        settle(zrecv.at[q], pz_send.at[q])
+        return carry
+
+    lax.fori_loop(0, CHUNKS, drain_z, 0)
+
+    cp_copy.wait()
     pooled = pool[0] + pool[1]
     for b in range(2):
         scale = 1.0 / (
@@ -474,45 +510,7 @@
     normed = centred / jnp.sqrt(variance + epsilon)
     chosen_rows = xrow[...].astype(F32) + xbuf[...].astype(F32)
     mixed_ref[...] = (normed * gates[...] + chosen_rows).astype(BF16)
-
-    x_copy.wait_send()
-    m_copy.wait_send()
-    cp_copy.wait_send()
     a_copy.wait_send()
-
-    @pl.when(holds)
-    def _():
-        for j in range(2):
-            for high in range(2):
-                wx_copy(j, high, 1).wait_send()
-                wx_copy(j, high, XS - 1).wait_send()
-                wf_copy(j, 1 - own_kv, high).wait_send()
-
-    @pl.when(jnp.logical_not(holds))
-    def _():
-        for j in range(2):
-            for high in range(2):
-                wh_copy(j, 0, high).wait_send()
-                for kv in range(2):
-                    wf_copy(j, kv, high).wait_send()
-
-    for d in range(1, zs):
-        qz_copy(d).wait_send()
-        cz_copy(d).wait_send()
-    for d in range(1, YS):
-        cy_copy(d).wait_send()
-    for d in range(zs):
-        for e in range(1, YS):
-            qy_copy(d, e).wait_send()
-
-    def drain(q, carry):
-        for d in range(1, YS):
-            py_copy(q, d).wait_send()
-        for d in range(1, zs):
-            pz_copy(q, d).wait_send()
-        return carry
-
-    lax.fori_loop(0, CHUNKS, drain, 0)
 
 
 def place_kernel(scores_ref, mixed_ref, selt_ref, coarse_ref, fine_ref):
@@ -571,17 +569,17 @@
         dma((2, 2, 2)),
         dma((zs - 1,)),
         dma((zs - 1,)),
-        dma((zs, YS - 1)),
-        dma((zs, YS - 1)),
-        dma((YS - 1,)),
-        dma((YS - 1,)),
-        dma((zs - 1,)),
-        dma((zs - 1,)),
+        dma((1,)),
+        dma((1,)),
+        dma((1,)),
+        dma((1,)),
+        dma((1,)),
+        dma((1,)),
         dma((2,)),
-        dma((CHUNKS, YS - 1)),
-        dma((CHUNKS, YS - 1)),
-        dma((CHUNKS, zs - 1)),
-        dma((CHUNKS, zs - 1)),
+        dma((CHUNKS,)),
+        dma((CHUNKS,)),
+        dma((CHUNKS,)),
+        dma((CHUNKS,)),
         dma((2,)),
         pltpu.SemaphoreType.REGULAR((zs // 2, 2)),
     ]

time: 54.3 us -> 49.4 us (0.910)
  Pallas kernels: 53.5 us -> 48.6 us
    pallas_call x1, Pallas kernels: 51.6 us -> 46.7 us  [local(): pl.pallas_call(functools.partial(kernel, zs), out_shape=(jax.ShapeDtypeSt...]
where the time goes in v4:
time: 49.4 us; the launch traced here: 49.2 us
  Pallas kernels  48.6 us (98%)
  between operations  0.64 us (1%)
    pallas_call x1, Pallas kernels, local(): pl.pallas_call(functools.partial(kernel, zs), out_shape=(jax.ShapeDtypeSt...  46.7 us
    pallas_call x1, Pallas kernels, local(): pl.pallas_call(place_kernel, out_shape=(jax.ShapeDtypeStruct((users, entr...  1.92 us

profile of v4, /device:TPU:1, one launch (start us, length us, event | category | flops | bytes accessed | tf_op | source)
XLA Modules:
  0.0 49.2 jit_solution(15368023621083662557)
XLA Ops:
  0.6 46.7 %shard_map.95 = (f32[2,128]{1,0:T(2,128)}, bf16[16,1024]{1,0:T(8,128)(2,1)}, bf16[2,128,16]{2,1,0:T(8,128)(2,1)}) custom-call(bf16[2,512,1024]{2,1,0:T(8,128)(2,1)} %m_hbm.1, bf16[2,128,1024]{2,1,0:T(8,128)(2,1)} %cand_hbm.1, bf16[1024,2048]{1,0:T(8,128)(2,1)} %wc_hbm.1, bf16[1024,512]{1,0:T(8,128)(2,1)} %wm_hbm.1, bf16[1024,1024]{1,0:T(8,128)(2,1)} %wco_hbm.1, ...), custom_call_target="tpu_custom_call" | custom-call | flops 6499999744 | bytes 12000000 | tf_op jit(solution)/shard_map/pallas_call | solution.py:587
  47.3 1.9 %shard_map.96 = (f32[2,128]{1,0:T(2,128)}, bf16[2,128,1024]{2,1,0:T(8,128)(2,1)}) custom-call(f32[2,128]{1,0:T(2,128)} %get-tuple-element.5.scores_ref, bf16[16,1024]{1,0:T(8,128)(2,1)} %get-tuple-element.6.mixed_ref, bf16[2,128,16]{2,1,0:T(8,128)(2,1)} %get-tuple-element.7.selt_ref), custom_call_target="tpu_custom_call" | custom-call | tf_op jit(solution)/shard_map/pallas_call | solution.py:605

commit v5 on v4

--- a/solution.py
+++ b/solution.py
@@ -209,10 +209,10 @@
 
     def wf_copy(j, kv, high):
         half_ = part(2 * colour + j, kv, high)
-        if j == 0:
-            device = ypeer(1 + high * (YS - 2))
-        else:
-            device = zpeer(1 + high * (zs - 2))
+        on_y = (kv == 0) if j == 0 else False
+        y_peer = ypeer(1 + high * (YS - 2))
+        z_peer = zpeer(1 + high * (zs - 2))
+        device = (u, jnp.where(on_y, y_peer[1], z_peer[1]))
         return remote(
             half_, half_, wf_send.at[j, kv, high], wf_recv.at[j, kv, high], device
         )
@@ -241,11 +241,14 @@
                 ).wait_recv()
                 wf_copy(j, 1 - own_kv, high).start()
 
+    hear(0)
+    tell(1, zpeer, zs)
     x_copy.wait_recv()
+    for r in range(1, rounds - 1):
+        hear(r)
+        tell(r + 1, zpeer, zs)
     rows = xrow[...].astype(F32) + xbuf[...].astype(F32)
     xrow2 = rows.astype(BF16)
-    hear(0)
-    tell(1, zpeer, zs)
     l_wq.wait()
     queries = silu(dot(xrow2, wq[...])).astype(BF16)
     qbuf[y, z] = (queries.astype(F32) * (0.5 / math.sqrt(2 * half // HEADS))).astype(BF16)
@@ -263,28 +266,21 @@
         for e in range(1, YS):
             qy_copy(d, e).start()
 
-    for d in (1, zs - 1, 2, zs - 2):
+    hear(rounds - 1)
+    for d in sorted(range(1, zs), key=lambda d: -min(d, zs - d)):
         qz_copy(d).start()
-    near_relay(0, 0)
-    for r in range(1, rounds):
-        hear(r)
-        if r + 1 < rounds:
-            tell(r + 1, zpeer, zs)
-        for d in sorted({r + 2, zs - r - 2}):
-            qz_copy(d).start()
     hear(rounds)
     qy_relay(0)
+    near_relay(0, 0)
     near_relay(0, 1)
-    l_wg.wait()
-    gates[...] = silu(dot(xrow2, wg[...]))
     qy_relay(1)
     qy_relay(zs - 1)
     near_relay(1, 0)
+    near_relay(1, 1)
     far_relay(0)
-    near_relay(1, 1)
-    for d in (2, zs - 2):
-        qy_relay(d)
     far_relay(1)
+    qy_relay(2)
+    qy_relay(zs - 2)
     for d in range(3, zs - 2):
         qy_relay(d)
 
@@ -308,11 +304,6 @@
         return carry
 
     lax.fori_loop(0, 2, own_chunk, 0)
-
-    l_wco.wait()
-    for b in range(2):
-        hidden = dot(cand[b], wco[...])
-        pre[b] = silu(hidden[:, :half]) * hidden[:, half:]
 
     live_row = lax.broadcasted_iota(jnp.int32, (rows16, hist), 0)
     live_col = lax.broadcasted_iota(jnp.int32, (rows16, hist), 1)
@@ -439,6 +430,11 @@
     settle(others, qy_send.at[0])
     settle(csy, cy_send.at[0])
 
+    l_wco.wait()
+    for b in range(2):
+        hidden = dot(cand[b], wco[...])
+        pre[b] = silu(hidden[:, :half]) * hidden[:, half:]
+
     settle(csz, cz_recv.at[0])
     packed = cs[1]
     for d in range(1, zs):
@@ -461,6 +457,10 @@
         return carry
 
     lax.fori_loop(0, CHUNKS, after, 0)
+
+    l_wg.wait()
+    chosen_rows = xrow[...].astype(F32) + xbuf[...].astype(F32)
+    gates[...] = silu(dot(chosen_rows.astype(BF16), wg[...]))
 
     def drain(q, carry):
         settle(yrecv.at[q], py_send.at[q])

time: 49.4 us -> 47.7 us (0.966)
  Pallas kernels: 48.6 us -> 46.9 us
    pallas_call x1, Pallas kernels: 46.7 us -> 45 us  [local(): pl.pallas_call(functools.partial(kernel, zs), out_shape=(jax.ShapeDtypeSt...]
where the time goes in v5:
time: 47.7 us; the launch traced here: 47.5 us
  Pallas kernels  46.9 us (98%)
  between operations  0.64 us (1%)
    pallas_call x1, Pallas kernels, local(): pl.pallas_call(functools.partial(kernel, zs), out_shape=(jax.ShapeDtypeSt...  45 us
    pallas_call x1, Pallas kernels, local(): pl.pallas_call(place_kernel, out_shape=(jax.ShapeDtypeStruct((users, entr...  1.93 us

profile of v5, /device:TPU:1, one launch (start us, length us, event | category | flops | bytes accessed | tf_op | source)
XLA Modules:
  0.0 47.5 jit_solution(10701644529666759330)
XLA Ops:
  0.6 45.0 %shard_map.95 = (f32[2,128]{1,0:T(2,128)}, bf16[16,1024]{1,0:T(8,128)(2,1)}, bf16[2,128,16]{2,1,0:T(8,128)(2,1)}) custom-call(bf16[2,512,1024]{2,1,0:T(8,128)(2,1)} %m_hbm.1, bf16[2,128,1024]{2,1,0:T(8,128)(2,1)} %cand_hbm.1, bf16[1024,2048]{1,0:T(8,128)(2,1)} %wc_hbm.1, bf16[1024,512]{1,0:T(8,128)(2,1)} %wm_hbm.1, bf16[1024,1024]{1,0:T(8,128)(2,1)} %wco_hbm.1, ...), custom_call_target="tpu_custom_call" | custom-call | flops 6499999744 | bytes 12000000 | tf_op jit(solution)/shard_map/pallas_call | solution.py:587
  45.6 1.9 %shard_map.96 = (f32[2,128]{1,0:T(2,128)}, bf16[2,128,1024]{2,1,0:T(8,128)(2,1)}) custom-call(f32[2,128]{1,0:T(2,128)} %get-tuple-element.5.scores_ref, bf16[16,1024]{1,0:T(8,128)(2,1)} %get-tuple-element.6.mixed_ref, bf16[2,128,16]{2,1,0:T(8,128)(2,1)} %get-tuple-element.7.selt_ref), custom_call_target="tpu_custom_call" | custom-call | tf_op jit(solution)/shard_map/pallas_call | solution.py:605

commit v6 on v5

--- a/solution.py
+++ b/solution.py
@@ -81,6 +81,8 @@
             device_id=device, device_id_type=MESH,
         )
 
+    far_first = sorted(range(1, zs), key=lambda d: -min(d, zs - d))
+
     def settle(ref, sem):
         pltpu.make_async_copy(ref, ref, sem).wait()
 
@@ -124,6 +126,42 @@
     l_wg.start()
     l_wco.start()
     l_avg.start()
+
+    pl.semaphore_wait(barrier, 7)
+
+    def tell(r, peer, size):
+        for side, d in ((0, 1), (1, size - 1)):
+            pl.semaphore_signal(
+                far_sem.at[r, side], inc=1, device_id=peer(d), device_id_type=MESH
+            )
+
+    def hear(r):
+        for side in range(2):
+            pl.semaphore_wait(far_sem.at[r, side], 1)
+
+    rounds = zs // 2 - 1
+    tell(0, zpeer, zs)
+    tell(rounds, ypeer, YS)
+
+    depth = wbuf.shape[2] // 2
+
+    def part(q, kv, high):
+        return wbuf.at[q, kv, pl.ds(pl.multiple_of(high * depth, depth), depth)]
+
+    def wx_copy(j, high, d):
+        half_ = part(2 * colour + j, own_kv, high)
+        return remote(
+            half_, half_, wx_send.at[j, high, d // 2], wx_recv.at[j, high, own_kv], xpeer(d)
+        )
+
+    @pl.when(holds)
+    def _():
+        for i in range(2):
+            for j in range(2):
+                if i == 0:
+                    wl_copy(2 * colour + j).wait()
+                wx_copy(j, i, 1).start()
+                wx_copy(j, 1 - i, XS - 1).start()
 
     rows16 = 2 * SLOTS
     ones = jnp.ones((rows16, idx_ref.shape[1]), BF16)
@@ -158,47 +196,11 @@
     found = dot(sel[0], cand[0]) + dot(sel[1], cand[1])
     xrow[...] = found.astype(BF16)
 
-    pl.semaphore_wait(barrier, 7)
-
-    def tell(r, peer, size):
-        for side, d in ((0, 1), (1, size - 1)):
-            pl.semaphore_signal(
-                far_sem.at[r, side], inc=1, device_id=peer(d), device_id_type=MESH
-            )
-
-    def hear(r):
-        for side in range(2):
-            pl.semaphore_wait(far_sem.at[r, side], 1)
-
-    rounds = zs // 2 - 1
-    tell(0, zpeer, zs)
-    tell(rounds, ypeer, YS)
-
     x_copy = remote(xrow, xbuf, x_sem.at[0], x_sem.at[1], sibling)
     x_copy.start()
 
     m_copy = remote(m_hbm, mall.at[:, c], m_sem.at[0], m_sem.at[1], sibling)
     m_copy.start()
-
-    depth = wbuf.shape[2] // 2
-
-    def part(q, kv, high):
-        return wbuf.at[q, kv, pl.ds(pl.multiple_of(high * depth, depth), depth)]
-
-    def wx_copy(j, high, d):
-        half_ = part(2 * colour + j, own_kv, high)
-        return remote(
-            half_, half_, wx_send.at[j, high, d // 2], wx_recv.at[j, high, own_kv], xpeer(d)
-        )
-
-    @pl.when(holds)
-    def _():
-        for i in range(2):
-            for j in range(2):
-                if i == 0:
-                    wl_copy(2 * colour + j).wait()
-                wx_copy(j, i, 1).start()
-                wx_copy(j, 1 - i, XS - 1).start()
 
     def wh_copy(j, kv, high):
         half_ = part(2 * colour + j, kv, high)
@@ -263,11 +265,11 @@
     def qy_relay(d):
         if d > 0:
             qz_copy(d).wait_recv()
-        for e in range(1, YS):
+        for e in (2, 1, YS - 1):
             qy_copy(d, e).start()
 
     hear(rounds - 1)
-    for d in sorted(range(1, zs), key=lambda d: -min(d, zs - d)):
+    for d in far_first:
         qz_copy(d).start()
     hear(rounds)
     qy_relay(0)
@@ -386,7 +388,7 @@
             pf[:, :, b * SLOTS:(b + 1) * SLOTS, :] = out.reshape(YS, zs, SLOTS, LANES)
         psend[q] = pf[...].astype(BF16)
         pown[q] = pf[y]
-        for d in range(1, YS):
+        for d in (2, 1, YS - 1):
             py_copy(q, d).start()
 
     def reduce_y(q):
@@ -397,7 +399,7 @@
         pown[q] = total_
         zsend[q] = total_.astype(BF16)
         zown[q] = pown[q, z]
-        for d in range(1, zs):
+        for d in far_first:
             pz_copy(q, d).start()
 
     def step(q, carry):

time: 47.7 us -> 47.3 us (level)
  no operation moved by 1% of the time
where the time goes in v6:
time: 47.3 us; the launch traced here: 47.1 us
  Pallas kernels  46.5 us (98%)
  between operations  0.64 us (1%)
    pallas_call x1, Pallas kernels, local(): pl.pallas_call(functools.partial(kernel, zs), out_shape=(jax.ShapeDtypeSt...  44.6 us
    pallas_call x1, Pallas kernels, local(): pl.pallas_call(place_kernel, out_shape=(jax.ShapeDtypeStruct((users, entr...  1.93 us

profile of v6, /device:TPU:1, one launch (start us, length us, event | category | flops | bytes accessed | tf_op | source)
XLA Modules:
  0.0 47.1 jit_solution(1018809178395518408)
XLA Ops:
  0.6 44.6 %shard_map.95 = (f32[2,128]{1,0:T(2,128)}, bf16[16,1024]{1,0:T(8,128)(2,1)}, bf16[2,128,16]{2,1,0:T(8,128)(2,1)}) custom-call(bf16[2,512,1024]{2,1,0:T(8,128)(2,1)} %m_hbm.1, bf16[2,128,1024]{2,1,0:T(8,128)(2,1)} %cand_hbm.1, bf16[1024,2048]{1,0:T(8,128)(2,1)} %wc_hbm.1, bf16[1024,512]{1,0:T(8,128)(2,1)} %wm_hbm.1, bf16[1024,1024]{1,0:T(8,128)(2,1)} %wco_hbm.1, ...), custom_call_target="tpu_custom_call" | custom-call | flops 6499999744 | bytes 12000000 | tf_op jit(solution)/shard_map/pallas_call | solution.py:589
  45.2 1.9 %shard_map.96 = (f32[2,128]{1,0:T(2,128)}, bf16[2,128,1024]{2,1,0:T(8,128)(2,1)}) custom-call(f32[2,128]{1,0:T(2,128)} %get-tuple-element.5.scores_ref, bf16[16,1024]{1,0:T(8,128)(2,1)} %get-tuple-element.6.mixed_ref, bf16[2,128,16]{2,1,0:T(8,128)(2,1)} %get-tuple-element.7.selt_ref), custom_call_target="tpu_custom_call" | custom-call | tf_op jit(solution)/shard_map/pallas_call | solution.py:607

commit v7 on v6

--- a/solution.py
+++ b/solution.py
@@ -406,7 +406,8 @@
         compute(q)
         return carry
 
-    lax.fori_loop(0, CHUNKS, step, 0)
+    for q in range(CHUNKS):
+        step(q, 0)
 
     x_copy.wait_send()
     m_copy.wait_send()

time: 47.3 us -> 47.5 us (level)
  no operation moved by 1% of the time
where the time goes in v7:
time: 47.5 us; the launch traced here: 47.3 us
  Pallas kernels  46.7 us (98%)
  between operations  0.64 us (1%)
    pallas_call x1, Pallas kernels, local(): pl.pallas_call(functools.partial(kernel, zs), out_shape=(jax.ShapeDtypeSt...  44.7 us
    pallas_call x1, Pallas kernels, local(): pl.pallas_call(place_kernel, out_shape=(jax.ShapeDtypeStruct((users, entr...  1.93 us

profile of v7, /device:TPU:1, one launch (start us, length us, event | category | flops | bytes accessed | tf_op | source)
XLA Modules:
  0.0 47.3 jit_solution(10635227732071237345)
XLA Ops:
  0.6 44.7 %shard_map.95 = (f32[2,128]{1,0:T(2,128)}, bf16[16,1024]{1,0:T(8,128)(2,1)}, bf16[2,128,16]{2,1,0:T(8,128)(2,1)}) custom-call(bf16[2,512,1024]{2,1,0:T(8,128)(2,1)} %m_hbm.1, bf16[2,128,1024]{2,1,0:T(8,128)(2,1)} %cand_hbm.1, bf16[1024,2048]{1,0:T(8,128)(2,1)} %wc_hbm.1, bf16[1024,512]{1,0:T(8,128)(2,1)} %wm_hbm.1, bf16[1024,1024]{1,0:T(8,128)(2,1)} %wco_hbm.1, ...), custom_call_target="tpu_custom_call" | custom-call | flops 6499999744 | bytes 12000000 | tf_op jit(solution)/shard_map/pallas_call | solution.py:590
  45.4 1.9 %shard_map.96 = (f32[2,128]{1,0:T(2,128)}, bf16[2,128,1024]{2,1,0:T(8,128)(2,1)}) custom-call(f32[2,128]{1,0:T(2,128)} %get-tuple-element.5.scores_ref, bf16[16,1024]{1,0:T(8,128)(2,1)} %get-tuple-element.6.mixed_ref, bf16[2,128,16]{2,1,0:T(8,128)(2,1)} %get-tuple-element.7.selt_ref), custom_call_target="tpu_custom_call" | custom-call | tf_op jit(solution)/shard_map/pallas_call | solution.py:608
